TPU v7x, 128 devices: a whole 4x4x4 slice. The times are simulated.
128 devices in a mesh: dp: 8 (over x, core), fsdp: 16 (over z, y).
Axes of the slice: x: 4, y: 4, z: 4, core: 2. Of those that a mesh axis runs over, the one named last changes fastest.
Arguments:
- gradients: bfloat16 [8, 128, 512, 512], P('dp', None, 'fsdp')
- block_owner: int32 [128], replicated, may hold values from 0 to 127, as said below
- left_stat: float32 [256, 512, 512], P(('dp', 'fsdp')), may hold values from -6 to 6
- right_stat: float32 [256, 512, 512], P(('dp', 'fsdp')), may hold values from -6 to 6
- root_left: bfloat16 [256, 512, 512], P(('dp', 'fsdp'))
- root_right: bfloat16 [256, 512, 512], P(('dp', 'fsdp'))
- moment_first: float32 [128, 512, 512], P('dp', 'fsdp'), may hold values from -0.75 to 0.75
- moment_second: float32 [128, 512, 512], P('dp', 'fsdp')
Outputs:
- update: bfloat16 [128, 512, 512], P('dp', 'fsdp')
- moment_first_new: float32 [128, 512, 512], P('dp', 'fsdp')
- moment_second_new: float32 [128, 512, 512], P('dp', 'fsdp')
- left_new: float32 [256, 512, 512], P(('dp', 'fsdp'))
- right_new: float32 [256, 512, 512], P(('dp', 'fsdp'))
Inputs may be any that keep to these rules, and one draw needn't show every extreme that they name: Block b's statistics and roots belong to device block_owner[b], devices numbered dp-major over dp and fsdp; block b's owner has dp index b // 16; each device owns at most 2 blocks and in every dp row some device owns exactly 2.
All inputs are finite; a program needn't handle non-finite values.
Results may differ from a plain program's by a relative error of at most 0.029.
Values may be sent and summed in bfloat16 or wider, within the bound.
A program may use at most 128 MiB of HBM per device.

v0:
```python
import jax
import jax.numpy as jnp
from jax import lax
from jax.sharding import PartitionSpec as P


def slot_ranking(block_owner):
    count = block_owner.shape[0]
    matches = block_owner[:, None] == block_owner[None, :]
    earlier = jnp.arange(count)[None, :] < jnp.arange(count)[:, None]
    return jnp.sum(jnp.where(matches & earlier, 1, 0), axis=1).astype(jnp.int32)


def shards(
    gradients,
    block_owner,
    left_stat,
    right_stat,
    root_left,
    root_right,
    moment_first,
    moment_second,
):
    dp_count = lax.axis_size("dp")
    fsdp_count = lax.axis_size("fsdp")
    device_count = dp_count * fsdp_count
    slot_count = left_stat.shape[0]
    block_count = block_owner.shape[0]
    strip_rows = gradients.shape[2]
    columns = gradients.shape[3]
    per_group = block_count // dp_count
    row_slots = fsdp_count * slot_count
    row_dp = lax.axis_index("dp")
    position = block_owner * slot_count + slot_ranking(block_owner)
    candidates = jnp.arange(device_count * slot_count, dtype=jnp.int32)
    matches = position[None, :] == candidates[:, None]
    filled = jnp.any(matches, axis=1)
    source = jnp.sum(
        jnp.where(matches, jnp.arange(block_count, dtype=jnp.int32)[None, :], 0), axis=1
    )
    partial_value = gradients[0]
    reduced = lax.psum_scatter(
        partial_value.astype(jnp.float32).astype(jnp.bfloat16),
        "dp",
        scatter_dimension=0,
        tiled=True,
    )
    row_source = lax.dynamic_slice_in_dim(source, row_dp * row_slots, row_slots)
    row_filled = lax.dynamic_slice_in_dim(filled, row_dp * row_slots, row_slots)
    offset = jnp.clip(row_source - row_dp * per_group, 0, per_group - 1)
    outgoing = jnp.where(row_filled[:, None, None], reduced[offset], 0)
    block_grad = lax.all_to_all(
        outgoing.reshape(fsdp_count, slot_count, strip_rows, columns),
        "fsdp",
        split_axis=0,
        concat_axis=0,
        tiled=True,
    )
    block_grad = jnp.moveaxis(block_grad, 1, 0).reshape(
        slot_count, fsdp_count * strip_rows, columns
    )
    gram_left = jnp.einsum(
        "sik,sjk->sij", block_grad, block_grad, preferred_element_type=jnp.float32
    )
    gram_right = jnp.einsum(
        "ski,skj->sij", block_grad, block_grad, preferred_element_type=jnp.float32
    )
    left_new = 0.95 * left_stat + 0.05 * gram_left
    right_new = 0.95 * right_stat + 0.05 * gram_right
    left_product = jnp.einsum(
        "sik,skj->sij", root_left, block_grad, preferred_element_type=jnp.float32
    )
    direction = jnp.einsum(
        "sik,skj->sij",
        left_product,
        root_right.astype(jnp.float32),
        precision=lax.Precision.HIGHEST,
    ).astype(jnp.bfloat16)
    pieces = jnp.moveaxis(direction.reshape(slot_count, fsdp_count, strip_rows, columns), 1, 0)
    returned = lax.all_to_all(pieces, "fsdp", split_axis=0, concat_axis=0, tiled=True).reshape(
        row_slots, strip_rows, columns
    )
    local_positions = (
        lax.dynamic_slice_in_dim(position, row_dp * per_group, per_group) - row_dp * row_slots
    )
    direction_strip = returned[local_positions].astype(jnp.float32)
    grad_float = reduced.astype(jnp.float32)
    moment_first_new = 0.9 * moment_first + 0.1 * grad_float
    moment_second_new = 0.95 * moment_second + 0.05 * grad_float * grad_float
    adam = moment_first_new / (jnp.sqrt(moment_second_new) + 1e-08)
    adam_part = jnp.sum(adam * adam, axis=(1, 2))
    direction_part = jnp.sum(direction_strip * direction_strip, axis=(1, 2))
    adam_sq, direction_sq = lax.psum((adam_part, direction_part), "fsdp")
    graft_scale = jnp.sqrt(adam_sq / (direction_sq + 1e-06))
    update = (-graft_scale[:, None, None] * direction_strip).astype(jnp.bfloat16)
    return (update, moment_first_new, moment_second_new, left_new, right_new)


def solution(mesh):
    placed = (
        P("dp", None, "fsdp", None),
        P(),
        P(("dp", "fsdp"), None, None),
        P(("dp", "fsdp"), None, None),
        P(("dp", "fsdp"), None, None),
        P(("dp", "fsdp"), None, None),
        P("dp", "fsdp", None),
        P("dp", "fsdp", None),
    )
    return jax.shard_map(
        shards,
        mesh=mesh,
        in_specs=placed,
        out_specs=(
            P("dp", "fsdp", None),
            P("dp", "fsdp", None),
            P("dp", "fsdp", None),
            P(("dp", "fsdp"), None, None),
            P(("dp", "fsdp"), None, None),
        ),
        check_vma=False,
    )
```

profile of v0, /device:TPU:6, one launch (start us, length us, event | category | flops | bytes accessed | tf_op | source)
XLA Modules:
  0.0 150.1 jit_solution(6620832489637801329)
XLA Ops:
  7.2 0.0 copy-start
  7.2 0.0 reduce-scatter.2.cloned.1.call-start
  7.2 0.0 copy-start.5
  7.2 0.7 reduce-scatter.2.cloned.1.call-update
  7.9 0.0 copy-done.5
  8.0 0.2 select_reduce_fusion.1
  8.1 0.1 fusion.4
  8.3 0.1 dynamic_slice.9
  8.3 0.1 broadcast_in_dim.51
  8.4 0.1 select_reduce_fusion
  8.6 0.1 compare_select_fusion.1
  8.7 38.3 %reduce-scatter.2.cloned.1.call-done = bf16[16,32,512]{2,1,0:T(8,128)(2,1)} async-done(((bf16[128,32,512]{2,1,0:T(8,128)(2,1)}), bf16[16,32,512]{2,1,0:T(8,128)(2,1)}) %reduce-scatter.2.cloned.1.call-update) | async-done | bytes 524304 | tf_op jit(solution)/shard_map/reduce_scatter | solution.py:42
  47.0 1.7 %gather_fusion = bf16[32,32,512]{2,1,0:T(8,128)(2,1)S(1)} fusion(bf16[16,32,512]{2,1,0:T(8,128)(2,1)} %reduce-scatter.2.cloned.1.call-done, s32[1024]{0:T(1024)S(1)} %pad_clamp_fusion.1), kind=kCustom, calls=%fused_computation | custom fusion | bytes 2097280 | tf_op jit(solution)/shard_map/gather | solution.py:51
  48.6 1.1 broadcast_select_fusion
  49.7 7.0 %all-to-all-start = ((bf16[16,2,32,512]{3,2,1,0:T(8,128)(2,1)}), bf16[16,2,32,512]{3,2,1,0:T(8,128)(2,1)S(1)}, u32[]{:S(2)}, u32[]{:S(2)}) async-start(bf16[16,2,32,512]{3,2,1,0:T(8,128)(2,1)} %broadcast_select_fusion), calls=%async_computation.1 | async-start | bytes 2097152 | tf_op jit(solution)/shard_map/all_to_all | solution.py:52
  56.7 0.1 compare_select_fusion
  56.8 19.2 %all-to-all-done = bf16[16,2,32,512]{3,2,1,0:T(8,128)(2,1)S(1)} async-done(((bf16[16,2,32,512]{3,2,1,0:T(8,128)(2,1)}), bf16[16,2,32,512]{3,2,1,0:T(8,128)(2,1)S(1)}, u32[]{:S(2)}, u32[]{:S(2)}) %all-to-all-start) | async-done | bytes 1048608 | tf_op jit(solution)/shard_map/all_to_all | solution.py:52
  76.0 0.1 copy.31
  76.1 0.0 copy-done
  76.1 0.0 copy-start.4
  76.1 0.7 fusion.8
  76.8 0.5 copy-done.4
  77.3 1.8 %convolution_convert_fusion = bf16[2,512,512]{2,1,0:T(8,128)(2,1)S(1)} fusion(f32[2,512,512]{1,2,0:T(8,128)S(1)} %fusion.8, bf16[2,512,512]{2,1,0:T(8,128)(2,1)S(1)} %copy-done.4), kind=kOutput, calls=%fused_computation.5 | convolution fusion | flops 3221749760 | bytes 4194304 | tf_op jit(solution)/shard_map/sik,skj->sij/dot_general | solution.py:73
  79.1 0.0 copy-start.1
  79.1 1.1 copy.40
  80.3 4.3 %all-to-all-start.1 = ((bf16[16,2,32,512]{3,2,1,0:T(8,128)(2,1)}), bf16[16,2,32,512]{3,2,1,0:T(8,128)(2,1)}, u32[]{:S(2)}, u32[]{:S(2)}) async-start(bf16[16,2,32,512]{3,2,1,0:T(8,128)(2,1)} %bitcast.23), calls=%async_computation.2 | async-start | bytes 2097152 | tf_op jit(solution)/shard_map/all_to_all | solution.py:80
  84.6 0.0 copy-done.1
  84.7 0.0 copy-start.2
  84.7 3.7 %multiply_reduce_fusion = (f32[16]{0:T(128)S(1)}, f32[16,32,512]{2,1,0:T(8,128)}, f32[16,32,512]{2,1,0:T(8,128)}) fusion(bf16[16,32,512]{2,1,0:T(8,128)(2,1)S(1)} %copy-done.1, f32[16,32,512]{2,1,0:T(8,128)} %param.15, f32[16,32,512]{2,1,0:T(8,128)} %param.14), kind=kLoop, calls=%fused_computation.14 | loop fusion | flops 3145712 | bytes 4718656 | tf_op jit(solution)/shard_map/reduce_sum | solution.py:91
  88.3 0.0 copy-done.2
  88.3 0.0 copy-start.3
  88.4 2.1 %multiply_add_fusion.1 = f32[2,512,512]{2,1,0:T(8,128)} fusion(f32[2,512,512]{2,1,0:T(8,128)S(1)} %copy-done.2, bf16[2,512,512]{2,1,0:T(8,128)(2,1)S(1)} %bitcast.19), kind=kOutput, calls=%fused_computation.3 | convolution fusion | flops 538443776 | bytes 5242880 | tf_op jit(solution)/shard_map/sik,sjk->sij/dot_general | solution.py:62
  90.5 0.0 copy-done.3
  90.5 2.2 %multiply_add_fusion = f32[2,512,512]{2,1,0:T(8,128)} fusion(f32[2,512,512]{2,1,0:T(8,128)S(1)} %copy-done.3, bf16[2,512,512]{2,1,0:T(8,128)(2,1)S(1)} %bitcast.20), kind=kOutput, calls=%fused_computation.2 | convolution fusion | flops 538443776 | bytes 5242880 | tf_op jit(solution)/shard_map/ski,skj->sij/dot_general | solution.py:65
  92.6 11.6 %all-to-all-done.1 = bf16[16,2,32,512]{3,2,1,0:T(8,128)(2,1)} async-done(((bf16[16,2,32,512]{3,2,1,0:T(8,128)(2,1)}), bf16[16,2,32,512]{3,2,1,0:T(8,128)(2,1)}, u32[]{:S(2)}, u32[]{:S(2)}) %all-to-all-start.1) | async-done | bytes 1048608 | tf_op jit(solution)/shard_map/all_to_all | solution.py:80
  104.2 1.8 %gather_fusion.1 = bf16[16,32,512]{2,1,0:T(8,128)(2,1)S(1)} fusion(bf16[32,32,512]{2,1,0:T(8,128)(2,1)} %bitcast.6, s32[1024]{0:T(1024)S(1)} %pad_clamp_fusion), kind=kCustom, calls=%fused_computation.1 | custom fusion | bytes 1048640 | tf_op jit(solution)/shard_map/gather | solution.py:86
  106.1 0.2 fusion.1
  106.3 36.0 %all-reduce = (f32[16]{0:T(128)S(1)}, f32[16]{0:T(128)S(1)}) all-reduce(f32[16]{0:T(128)S(1)} %get-tuple-element.7, f32[16]{0:T(128)S(1)} %fusion.1), channel_id=1, replica_groups=mesh['dp'=8,'fsdp'=16] {'fsdp'}, use_global_device_ids=true, to_apply=%region_2.3 | all-reduce | flops 32 | bytes 256 | tf_op jit(solution)/shard_map/psum | solution.py:93
  142.3 1.0 fusion.2
  (4 shorter events, 0.0 us)
Async XLA Ops:
  7.2 68.9 %copy-start = (bf16[2,512,512]{2,1,0:T(8,128)(2,1)S(1)}, bf16[2,512,512]{2,1,0:T(8,128)(2,1)}, u32[]{:S(2)}) copy-start(bf16[2,512,512]{2,1,0:T(8,128)(2,1)} %param.12) | copy-start | bytes 3145732
  7.2 39.8 %reduce-scatter.2.cloned.1.call-start = ((), (), s32[]{:S(2)}) async-start(), calls=%async_computation.3 | async-start | bytes 4718592 | tf_op jit(solution)/shard_map/reduce_scatter | solution.py:42
  7.2 0.7 copy-start.5
  49.7 26.2 %all-to-all-start = ((bf16[16,2,32,512]{3,2,1,0:T(8,128)(2,1)}), bf16[16,2,32,512]{3,2,1,0:T(8,128)(2,1)S(1)}, u32[]{:S(2)}, u32[]{:S(2)}) async-start(bf16[16,2,32,512]{3,2,1,0:T(8,128)(2,1)} %broadcast_select_fusion), calls=%async_computation.1 | async-start | bytes 2097152 | tf_op jit(solution)/shard_map/all_to_all | solution.py:52
  76.1 1.2 copy-start.4
  79.1 5.5 %copy-start.1 = (bf16[16,32,512]{2,1,0:T(8,128)(2,1)S(1)}, bf16[16,32,512]{2,1,0:T(8,128)(2,1)}, u32[]{:S(2)}) copy-start(bf16[16,32,512]{2,1,0:T(8,128)(2,1)} %reduce-scatter.2.cloned.1.call-done) | copy-start | bytes 1572868
  80.3 23.9 %all-to-all-start.1 = ((bf16[16,2,32,512]{3,2,1,0:T(8,128)(2,1)}), bf16[16,2,32,512]{3,2,1,0:T(8,128)(2,1)}, u32[]{:S(2)}, u32[]{:S(2)}) async-start(bf16[16,2,32,512]{3,2,1,0:T(8,128)(2,1)} %bitcast.23), calls=%async_computation.2 | async-start | bytes 2097152 | tf_op jit(solution)/shard_map/all_to_all | solution.py:80
  84.7 3.7 %copy-start.2 = (f32[2,512,512]{2,1,0:T(8,128)S(1)}, f32[2,512,512]{2,1,0:T(8,128)}, u32[]{:S(2)}) copy-start(f32[2,512,512]{2,1,0:T(8,128)} %param.10) | copy-start | bytes 6291460
  88.3 2.1 %copy-start.3 = (f32[2,512,512]{2,1,0:T(8,128)S(1)}, f32[2,512,512]{2,1,0:T(8,128)}, u32[]{:S(2)}) copy-start(f32[2,512,512]{2,1,0:T(8,128)} %param.11) | copy-start | bytes 6291460
Sparse Core Ops, SparseCore 0:
  10.4 36.5 reduce-scatter.1
where the time goes:
time: 151 us; the launch traced here: 150 us
  waiting for transfers between devices  69.7 us (46%)
  blocking collectives  36 us (24%)
  between operations  14.2 us (9%)
  starting transfers between devices  11.4 us (8%)
  matrix products  6.78 us (4%)
  other arithmetic  6.59 us (4%)
  local copies, waits for them, and re-layouts  5.45 us (4%)
    reduce_scatter x1, waiting for transfers between devices, shards(): lax.psum_scatter(partial_value.astype(jnp.float32).astype(jnp.bfloat16),...  38.3 us
    psum x1, blocking collectives, shards(): adam_sq, direction_sq = lax.psum((adam_part, direction_part), 'fsdp')  36 us
    all_to_all x1, waiting for transfers between devices, shards(): lax.all_to_all(outgoing.reshape(fsdp_count, slot_count, strip_rows, colum...  19.2 us
    all_to_all x1, waiting for transfers between devices, shards(): lax.all_to_all(pieces, 'fsdp', split_axis=0, concat_axis=0, tiled=True)  11.6 us
    all_to_all x1, starting transfers between devices, shards(): lax.all_to_all(outgoing.reshape(fsdp_count, slot_count, strip_rows, colum...  6.99 us
    all_to_all x1, starting transfers between devices, shards(): lax.all_to_all(pieces, 'fsdp', split_axis=0, concat_axis=0, tiled=True)  4.34 us
    reduce_sum x1, other arithmetic, shards(): adam_part = jnp.sum(adam * adam, axis=(1, 2))  3.68 us
  transfers between devices with their start and end apart: 3, of which 3 were waited for; matrix products, arithmetic and copies ran while one was open for 6% of the time, Pallas kernels for 0%

commit v1 on v0

v1 whole, which is shorter than its diff:
```python
import functools

import jax
import jax.numpy as jnp
from jax import lax
from jax.experimental import pallas as pl
from jax.experimental.pallas import tpu as pltpu
from jax.sharding import PartitionSpec as P

F32 = jnp.float32
BF16 = jnp.bfloat16
I32 = jnp.int32
CHUNKS = 4
SIDE = 4
NEAR = ((1, 0), (-1, 0), (0, 1), (0, -1), (1, 1), (-1, -1), (1, -1), (-1, 1))
LEGS = (
    (
        ((1, 1), (1, 1)),
        ((1, 1), (1, 0)),
        ((1, -1), (1, 0)),
        ((1, 1), (0, 1)),
        ((-1, 1), (0, 1)),
        ((1, 0), (1, 0)),
        ((0, 1), (0, 1)),
    ),
    (
        ((-1, -1), (-1, -1)),
        ((-1, 1), (-1, 0)),
        ((-1, -1), (-1, 0)),
        ((1, -1), (0, -1)),
        ((-1, -1), (0, -1)),
        ((-1, 0), (-1, 0)),
        ((0, -1), (0, -1)),
    ),
)


def exchange_kernel(
    owner_ref,
    grad_ref,
    root_left_ref,
    root_right_ref,
    first_ref,
    second_ref,
    left_ref,
    right_ref,
    update_out,
    first_out,
    second_out,
    left_out,
    right_out,
    owner,
    places,
    place,
    own,
    other,
    pair,
    relay_right,
    relay_left,
    from_left,
    from_right,
    reduced,
    outgoing,
    block,
    root_left,
    root_right,
    first,
    second,
    stat_left,
    stat_right,
    direction,
    returned,
    relayed,
    sums,
    all_sums,
    sizes,
    graft,
    update,
    place_sem,
    own_sem,
    load_sem,
    store_sem,
    core_send,
    core_recv,
    ring_send,
    ring_recv,
    owner_send,
    owner_recv,
    back_send,
    back_recv,
    relay_send,
    relay_recv,
    sums_send,
    sums_recv,
):
    lines, _, per_group, strip, columns = grad_ref.shape
    width = columns // CHUNKS
    half = per_group // 2
    slots, rows = block.shape[:2]
    ranks = rows // strip
    count = owner.shape[1]
    dp = lax.axis_index("dp")
    rank = lax.axis_index("fsdp")
    x = dp // 2
    core = dp % 2
    y = rank % SIDE
    z = rank // SIDE
    mate = x * 2 + (1 - core)
    ahead = (x + 1) % lines
    behind = (x + lines - 1) % lines
    across = (x + 2) % lines
    right = ahead * 2 + core
    left = behind * 2 + core
    chunks = range(CHUNKS)

    def cols(k):
        return pl.ds(k * width, width)

    def strip_rows(at):
        return pl.ds(pl.multiple_of(at * strip, strip), strip)

    sign = 1 - 2 * core

    def at_offset(dy, dz):
        target_y = (y + SIDE + sign * dy) % SIDE
        target_z = (z + SIDE + sign * dz) % SIDE
        return target_z * SIDE + target_y

    def each_target(visit):
        @pl.loop(0, SIDE)
        def _(turn):
            for index, (dy, shift) in enumerate(((1, 0), (3, 2), (2, 3), (0, 1))):
                dz = (turn + shift) % SIDE
                target = at_offset(dy, dz)
                if index < 3:
                    visit(target)
                else:
                    pl.when(turn < SIDE - 1)(functools.partial(visit, target))

    owner_load = pltpu.make_async_copy(owner_ref, owner, place_sem.at[0])
    owner_load.start()
    own_loads = []
    for k in chunks:
        load = pltpu.make_async_copy(
            grad_ref.at[:, core, :, :, cols(k)], own.at[k], own_sem.at[k]
        )
        load.start()
        own_loads.append(load)
    loads = [
        pltpu.make_async_copy(src, dst, load_sem.at[index])
        for index, (src, dst) in enumerate(
            (
                (root_left_ref, root_left),
                (root_right_ref, root_right),
                (first_ref, first),
                (second_ref, second),
                (left_ref, stat_left),
                (right_ref, stat_right),
            )
        )
    ]
    barrier = pltpu.get_barrier_semaphore()
    for partner in (mate, right, left):
        pl.semaphore_signal(barrier, inc=1, device_id={"dp": partner})

    @pl.loop(1, ranks)
    def _(step):
        pl.semaphore_signal(barrier, inc=1, device_id={"fsdp": (rank + step) % ranks})

    owner_load.wait()
    along = lax.broadcasted_iota(I32, (count, count), 1)
    down = lax.broadcasted_iota(I32, (count, count), 0)
    owner_row = owner[...]
    owner_all = jnp.broadcast_to(owner_row, (count, count)).astype(F32)
    owner_col = jnp.sum(jnp.where(along == down, owner_all, 0.0), axis=1, keepdims=True)
    same = owner_all == owner_col
    slot_row = jnp.sum(jnp.where(same & (down < along), 1.0, 0.0), axis=0, keepdims=True)
    slot_col = jnp.sum(jnp.where(same & (along < down), 1.0, 0.0), axis=1, keepdims=True)
    offset = (dp * (ranks * slots)).astype(F32)
    place_row = owner_row.astype(F32) * slots + slot_row - offset
    place_col = owner_col * slots + slot_col - offset
    number = (down - dp * per_group + 1).astype(F32)
    held_row = jnp.sum(
        jnp.where(along.astype(F32) == place_col, number, 0.0), axis=0, keepdims=True
    )
    places[0:1] = place_row.astype(I32)
    places[1:2] = held_row.astype(I32)
    place_copy = pltpu.make_async_copy(places, place, place_sem.at[1])
    place_copy.start()

    pl.semaphore_wait(barrier, ranks + 2)

    core_copies = []
    for k in chunks:
        copies = []
        for index, line in enumerate((across, ahead, behind, x)):
            copy = pltpu.make_async_remote_copy(
                src_ref=grad_ref.at[line, 1 - core, :, :, cols(k)],
                dst_ref=other.at[k, line],
                send_sem=core_send.at[k, index],
                recv_sem=core_recv.at[k, line],
                device_id={"dp": mate},
            )
            copy.start()
            copies.append(copy)
        core_copies.append(copies)
    place_copy.wait()

    def held(at):
        return place[1, at]

    def block_of(at):
        return jnp.clip(held(at) - 1, 0, per_group - 1)

    def place_of(index):
        return jnp.clip(place[0, dp * per_group + index], 0, ranks * slots - 1)

    def wait_core(k, line):
        ref = other.at[k, line]
        pltpu.make_async_copy(ref, ref, core_recv.at[k, line]).wait()

    def ring(k, index, src, dst, target):
        return pltpu.make_async_remote_copy(
            src_ref=src,
            dst_ref=dst,
            send_sem=ring_send.at[k, index],
            recv_sem=ring_recv.at[k, index],
            device_id={"dp": target},
        )

    ring_copies = [None] * CHUNKS
    low, high = pl.ds(0, half), pl.ds(half, half)

    def far_sums(k):
        copies = [
            ring(k, 0, pair.at[k, across, low], relay_right.at[k], right),
            ring(k, 1, pair.at[k, across, high], relay_left.at[k], left),
            ring(k, 2, pair.at[k, ahead, high], from_left.at[k, high], right),
            ring(k, 3, pair.at[k, behind, low], from_right.at[k, low], left),
            ring(k, 4, pair.at[k, ahead, low], from_left.at[k, low], right),
            ring(k, 5, pair.at[k, behind, high], from_right.at[k, high], left),
        ]
        ring_copies[k] = copies
        own_loads[k].wait()
        wait_core(k, across)
        pair[k, across] = own[k, across] + other[k, across]
        copies[0].start()
        copies[1].start()

    def near_sums(k):
        copies = ring_copies[k]
        wait_core(k, ahead)
        pair[k, ahead] = own[k, ahead] + other[k, ahead]
        copies[2].start()
        wait_core(k, behind)
        pair[k, behind] = own[k, behind] + other[k, behind]
        copies[3].start()

    def relay(k):
        copies = ring_copies[k]
        copies[0].wait_recv()
        pair[k, ahead, low] = pair[k, ahead, low] + relay_right[k]
        copies[4].start()
        copies[1].wait_recv()
        pair[k, behind, high] = pair[k, behind, high] + relay_left[k]
        copies[5].start()

    def finish(k):
        wait_core(k, x)
        total = own[k, x].astype(F32) + other[k, x].astype(F32)
        for copy in ring_copies[k][2:]:
            copy.wait_recv()
        total = total + from_left[k].astype(F32) + from_right[k].astype(F32)
        reduced[k] = total.astype(BF16)

        def visit(target):
            for slot in range(slots):
                outgoing[k, target, slot] = reduced[k, block_of(target * slots + slot)]
            pltpu.make_async_remote_copy(
                src_ref=outgoing.at[k, target],
                dst_ref=block.at[:, strip_rows(rank), cols(k)],
                send_sem=owner_send.at[k],
                recv_sem=owner_recv.at[k],
                device_id={"fsdp": target},
            ).start()

        each_target(visit)
        for slot in range(slots):
            block[slot, strip_rows(rank), cols(k)] = reduced[k, block_of(rank * slots + slot)]

    far_sums(0)
    near_sums(0)
    far_sums(1)
    relay(0)
    for load in loads:
        load.start()
    for k in chunks:
        if k + 1 < CHUNKS:
            near_sums(k + 1)
        if k + 2 < CHUNKS:
            far_sums(k + 2)
        if k + 1 < CHUNKS:
            relay(k + 1)
        finish(k)

    others = (ranks - 1) * strip

    def arrived(ref, sem):
        pltpu.make_async_copy(ref, ref, sem).wait()

    for k in chunks:
        arrived(block.at[:, pl.ds(0, others), cols(k)], owner_recv.at[k])
    loads[0].wait()
    loads[1].wait()

    for slot in range(slots):
        product = jnp.dot(root_left[slot], block[slot], preferred_element_type=F32)
        direction[slot] = jnp.dot(
            product.astype(BF16), root_right[slot], preferred_element_type=F32
        ).astype(BF16)

        for index, (first_leg, second_leg) in enumerate(LEGS[slot]):
            target = at_offset(first_leg[0] + second_leg[0], first_leg[1] + second_leg[1])
            pltpu.make_async_remote_copy(
                src_ref=direction.at[slot, strip_rows(target)],
                dst_ref=relayed.at[slot, index],
                send_sem=back_send.at[slot],
                recv_sem=relay_recv.at[slot, index],
                device_id={"fsdp": at_offset(*first_leg)},
            ).start()
        for offset in NEAR:
            target = at_offset(*offset)
            pltpu.make_async_remote_copy(
                src_ref=direction.at[slot, strip_rows(target)],
                dst_ref=returned.at[rank, slot],
                send_sem=back_send.at[slot],
                recv_sem=back_recv.at[slot],
                device_id={"fsdp": target},
            ).start()

    for slot in range(slots):
        for index, (first_leg, second_leg) in enumerate(LEGS[slot]):
            origin = at_offset(-first_leg[0], -first_leg[1])
            arrived(relayed.at[slot, index], relay_recv.at[slot, index])
            pltpu.make_async_remote_copy(
                src_ref=relayed.at[slot, index],
                dst_ref=returned.at[origin, slot],
                send_sem=relay_send.at[slot],
                recv_sem=back_recv.at[slot],
                device_id={"fsdp": at_offset(*second_leg)},
            ).start()

    for slot in range(slots):
        returned[rank, slot] = direction[slot, strip_rows(rank)]
        wide = direction[slot].astype(F32)
        wide = jnp.sum((wide * wide).reshape(-1, 8, columns), axis=0)
        sums[2 + slot] = functools.reduce(
            jnp.add, [wide[:, at : at + 128] for at in range(0, columns, 128)]
        )
    loads[2].wait()
    loads[3].wait()

    @pl.loop(0, per_group)
    def _(index):
        total = jnp.zeros((1, 128), F32)
        for k in chunks:
            grad = reduced[k, index].astype(F32)
            first_new = 0.9 * first[index, :, cols(k)] + 0.1 * grad
            second_new = 0.95 * second[index, :, cols(k)] + 0.05 * grad * grad
            first[index, :, cols(k)] = first_new
            second[index, :, cols(k)] = second_new
            adam = first_new / (jnp.sqrt(second_new) + 1e-08)
            part = jnp.sum(adam * adam, axis=0, keepdims=True)
            for at in range(0, width, 128):
                total = total + part[:, at : at + 128]
        sums[index // 8, pl.ds(index % 8, 1)] = total

    def send_sums(target):
        pltpu.make_async_remote_copy(
            src_ref=sums,
            dst_ref=all_sums.at[rank],
            send_sem=sums_send,
            recv_sem=sums_recv,
            device_id={"fsdp": target},
        ).start()

    each_target(send_sums)
    all_sums[rank] = sums[...]
    stores = [
        pltpu.make_async_copy(first, first_out, store_sem.at[0]),
        pltpu.make_async_copy(second, second_out, store_sem.at[1]),
    ]
    for store in stores:
        store.start()

    loads[4].wait()
    loads[5].wait()
    for stat, contract, index, out in ((stat_left, 1, 2, left_out), (stat_right, 0, 3, right_out)):
        for slot in range(slots):
            gram = lax.dot_general(
                block[slot],
                block[slot],
                (((contract,), (contract,)), ((), ())),
                preferred_element_type=F32,
            )
            used = held(rank * slots + slot) > 0
            stat[slot] = 0.95 * stat[slot] + 0.05 * jnp.where(used, gram, 0.0)
        store = pltpu.make_async_copy(stat, out, store_sem.at[index])
        store.start()
        stores.append(store)

    arrived(all_sums.at[pl.ds(0, ranks - 1)], sums_recv)
    for index in range(per_group):
        at = place_of(index)
        sizes[index] = all_sums[at // slots, 2 + at % slots]
    adam_sq = jnp.sum(all_sums[:, 0:2], axis=0).reshape(per_group, 128)
    adam_sq = jnp.sum(adam_sq, axis=1, keepdims=True)
    direction_sq = jnp.sum(jnp.sum(sizes[...], axis=1), axis=1, keepdims=True)
    graft[...] = jnp.broadcast_to(jnp.sqrt(adam_sq / (direction_sq + 1e-06)), graft.shape)

    for slot in range(slots):
        arrived(returned.at[pl.ds(0, ranks - 1), slot], back_recv.at[slot])

    @pl.loop(0, per_group)
    def _(index):
        at = place_of(index)
        scale = -graft[pl.ds(index, 1)]
        value = returned[at // slots, at % slots].astype(F32)
        update[index] = (value * jnp.concatenate([scale] * (columns // 128), axis=1)).astype(BF16)

    store = pltpu.make_async_copy(update, update_out, store_sem.at[4])
    store.start()
    stores.append(store)

    for k in chunks:
        for copy in core_copies[k] + ring_copies[k]:
            copy.wait_send()
        arrived(outgoing.at[k, pl.ds(0, ranks - 1)], owner_send.at[k])
    for slot in range(slots):
        arrived(direction.at[slot, pl.ds(0, others)], back_send.at[slot])
        arrived(relayed.at[slot], relay_send.at[slot])
    arrived(all_sums.at[pl.ds(0, ranks - 1)], sums_send)
    for store in stores:
        store.wait()


def exchange(block_owner, gradients, root_left, root_right, first, second, left, right, ranks):
    lines, _, per_group, strip, columns = gradients.shape
    slots, rows, _ = root_left.shape
    width = columns // CHUNKS
    half = per_group // 2
    anywhere = pl.BlockSpec(memory_space=pl.ANY)
    far = pl.BlockSpec(memory_space=pltpu.HBM)
    dma = pltpu.SemaphoreType.DMA
    vmem = pltpu.VMEM
    return pl.pallas_call(
        exchange_kernel,
        out_shape=(
            jax.ShapeDtypeStruct(first.shape, BF16),
            jax.ShapeDtypeStruct(first.shape, F32),
            jax.ShapeDtypeStruct(first.shape, F32),
            jax.ShapeDtypeStruct(left.shape, F32),
            jax.ShapeDtypeStruct(right.shape, F32),
        ),
        in_specs=[far] * 8,
        out_specs=(anywhere,) * 5,
        scratch_shapes=[
            vmem(block_owner.shape, I32),
            vmem((8, 128), I32),
            pltpu.SMEM((8, 128), I32),
            vmem((CHUNKS, lines, per_group, strip, width), BF16),
            vmem((CHUNKS, lines, per_group, strip, width), BF16),
            vmem((CHUNKS, lines, per_group, strip, width), BF16),
            vmem((CHUNKS, half, strip, width), BF16),
            vmem((CHUNKS, half, strip, width), BF16),
            vmem((CHUNKS, per_group, strip, width), BF16),
            vmem((CHUNKS, per_group, strip, width), BF16),
            vmem((CHUNKS, per_group, strip, width), BF16),
            vmem((CHUNKS, ranks, slots, strip, width), BF16),
            vmem((slots, rows, columns), BF16),
            vmem((slots, rows, columns), BF16),
            vmem((slots, rows, columns), BF16),
            vmem(first.shape, F32),
            vmem(first.shape, F32),
            vmem(left.shape, F32),
            vmem(right.shape, F32),
            vmem((slots, rows, columns), BF16),
            vmem((ranks, slots, strip, columns), BF16),
            vmem((slots, len(LEGS[0]), strip, columns), BF16),
            vmem((4, 8, 128), F32),
            vmem((ranks, 4, 8, 128), F32),
            vmem((per_group, 8, 128), F32),
            vmem((per_group, 128), F32),
            vmem((per_group, strip, columns), BF16),
            dma((2,)),
            dma((CHUNKS,)),
            dma((6,)),
            dma((5,)),
            dma((CHUNKS, 4)),
            dma((CHUNKS, 4)),
            dma((CHUNKS, 6)),
            dma((CHUNKS, 6)),
            dma((CHUNKS,)),
            dma((CHUNKS,)),
            dma((slots,)),
            dma((slots,)),
            dma((slots,)),
            dma((slots, len(LEGS[0]))),
            dma,
            dma,
        ],
        compiler_params=pltpu.CompilerParams(
            collective_id=0, has_side_effects=True, vmem_limit_bytes=40 * 2**20
        ),
        cost_estimate=pl.CostEstimate(
            flops=8 * slots * rows * rows * columns, bytes_accessed=18 * 2**20, transcendentals=0
        ),
        name="exchange",
    )(
        *(
            pltpu.with_memory_space_constraint(value, pltpu.HBM)
            for value in (
                block_owner,
                gradients,
                root_left,
                root_right,
                first,
                second,
                left,
                right,
            )
        )
    )


def publish_kernel(*refs):
    count = (len(refs) - 1) // 2
    sems = refs[-1]
    copies = [
        pltpu.make_async_copy(refs[index], refs[count + index], sems.at[index])
        for index in range(count)
    ]
    for copy in copies:
        copy.start()
    for copy in copies:
        copy.wait()


def publish(results):
    return pl.pallas_call(
        publish_kernel,
        out_shape=[jax.ShapeDtypeStruct(value.shape, value.dtype) for value in results],
        in_specs=[pl.BlockSpec(memory_space=pl.ANY)] * len(results),
        out_specs=[pl.BlockSpec(memory_space=pltpu.HBM)] * len(results),
        scratch_shapes=[pltpu.SemaphoreType.DMA((len(results),))],
        compiler_params=pltpu.CompilerParams(vmem_limit_bytes=2**20),
        name="publish",
    )(*(pltpu.with_memory_space_constraint(value, pltpu.VMEM) for value in results))


def shards(
    gradients,
    block_owner,
    left_stat,
    right_stat,
    root_left,
    root_right,
    moment_first,
    moment_second,
):
    dp_count = lax.axis_size("dp")
    ranks = lax.axis_size("fsdp")
    count = block_owner.shape[0]
    strip, columns = gradients.shape[2:]
    results = exchange(
        block_owner.reshape(1, count),
        gradients.reshape(dp_count // 2, 2, count // dp_count, strip, columns),
        root_left,
        root_right,
        moment_first,
        moment_second,
        left_stat,
        right_stat,
        ranks,
    )
    return tuple(publish(results))


def solution(mesh):
    placed = (
        P("dp", None, "fsdp", None),
        P(),
        P(("dp", "fsdp"), None, None),
        P(("dp", "fsdp"), None, None),
        P(("dp", "fsdp"), None, None),
        P(("dp", "fsdp"), None, None),
        P("dp", "fsdp", None),
        P("dp", "fsdp", None),
    )
    return jax.shard_map(
        shards,
        mesh=mesh,
        in_specs=placed,
        out_specs=(
            P("dp", "fsdp", None),
            P("dp", "fsdp", None),
            P("dp", "fsdp", None),
            P(("dp", "fsdp"), None, None),
            P(("dp", "fsdp"), None, None),
        ),
        check_vma=False,
    )
```

time: 151 us -> 60.1 us (0.40)
  the two profiles are of different devices: /device:TPU:6 before, /device:TPU:0 now
where the time goes in v1:
time: 60.1 us; the launch traced here: 59.8 us
  Pallas kernels  59.2 us (99%)
  between operations  0.64 us (1%)
    pallas_call x1, Pallas kernels, exchange(): pl.pallas_call(exchange_kernel, out_shape=(jax.ShapeDtypeStruct(first.sha...  56.2 us
    pallas_call x1, Pallas kernels, publish(): pl.pallas_call(publish_kernel, out_shape=[jax.ShapeDtypeStruct(value.shap...  2.92 us

profile of v1, /device:TPU:0, one launch (start us, length us, event | category | flops | bytes accessed | tf_op | source)
XLA Modules:
  0.0 59.8 jit_solution(17966045538820524089)
XLA Ops:
  0.6 56.2 %exchange.1 = (bf16[16,32,512]{2,1,0:T(8,128)(2,1)S(1)}, f32[16,32,512]{2,1,0:T(8,128)S(1)}, f32[16,32,512]{2,1,0:T(8,128)S(1)}, f32[2,512,512]{2,1,0:T(8,128)S(1)}, f32[2,512,512]{2,1,0:T(8,128)S(1)}) custom-call(s32[1,128]{1,0:T(1,128)} %bitcast.3, bf16[4,2,16,32,512]{4,3,2,1,0:T(8,128)(2,1)} %bitcast.2, bf16[2,512,512]{2,1,0:T(8,128)(2,1)} %root_left_ref.1, ...), custom_call_target="tpu_custom_call" | custom-call | flops 2147483648 | bytes 18874368 | tf_op jit(solution)/shard_map/exchange/pallas_call | solution.py:456
  56.9 2.9 %publish.1 = (bf16[16,32,512]{2,1,0:T(8,128)(2,1)}, f32[16,32,512]{2,1,0:T(8,128)}, f32[16,32,512]{2,1,0:T(8,128)}, f32[2,512,512]{2,1,0:T(8,128)}, f32[2,512,512]{2,1,0:T(8,128)}) custom-call(bf16[16,32,512]{2,1,0:T(8,128)(2,1)S(1)} %get-tuple-element.10.refs_0_, f32[16,32,512]{2,1,0:T(8,128)S(1)} %get-tuple-element.11.refs_1_, ...), custom_call_target="tpu_custom_call" | custom-call | tf_op jit(solution)/shard_map/publish/pallas_call | solution.py:550

commit v2 on v1

--- a/solution.py
+++ b/solution.py
@@ -14,25 +14,19 @@
 SIDE = 4
 NEAR = ((1, 0), (-1, 0), (0, 1), (0, -1), (1, 1), (-1, -1), (1, -1), (-1, 1))
 LEGS = (
-    (
-        ((1, 1), (1, 1)),
-        ((1, 1), (1, 0)),
-        ((1, -1), (1, 0)),
-        ((1, 1), (0, 1)),
-        ((-1, 1), (0, 1)),
-        ((1, 0), (1, 0)),
-        ((0, 1), (0, 1)),
-    ),
-    (
-        ((-1, -1), (-1, -1)),
-        ((-1, 1), (-1, 0)),
-        ((-1, -1), (-1, 0)),
-        ((1, -1), (0, -1)),
-        ((-1, -1), (0, -1)),
-        ((-1, 0), (-1, 0)),
-        ((0, -1), (0, -1)),
-    ),
+    ((1, 1), (1, 1)),
+    ((-1, 1), (-1, 0)),
+    ((-1, -1), (-1, 0)),
+    ((1, -1), (0, -1)),
+    ((-1, -1), (0, -1)),
+    ((1, 0), (1, 0)),
+    ((0, 1), (0, 1)),
 )
+
+
+def legs_of(slot):
+    sign = 1 - 2 * slot
+    return [tuple((sign * dy, sign * dz) for dy, dz in legs) for legs in LEGS]
 
 
 def exchange_kernel(
@@ -106,8 +100,9 @@
     y = rank % SIDE
     z = rank // SIDE
     mate = x * 2 + (1 - core)
-    ahead = (x + 1) % lines
-    behind = (x + lines - 1) % lines
+    sign = 1 - 2 * core
+    ahead = (x + lines + sign) % lines
+    behind = (x + lines - sign) % lines
     across = (x + 2) % lines
     right = ahead * 2 + core
     left = behind * 2 + core
@@ -118,8 +113,6 @@
 
     def strip_rows(at):
         return pl.ds(pl.multiple_of(at * strip, strip), strip)
-
-    sign = 1 - 2 * core
 
     def at_offset(dy, dz):
         target_y = (y + SIDE + sign * dy) % SIDE
@@ -264,7 +257,6 @@
         copies[1].wait_recv()
         pair[k, behind, high] = pair[k, behind, high] + relay_left[k]
         copies[5].start()
-
     def finish(k):
         wait_core(k, x)
         total = own[k, x].astype(F32) + other[k, x].astype(F32)
@@ -319,7 +311,7 @@
             product.astype(BF16), root_right[slot], preferred_element_type=F32
         ).astype(BF16)
 
-        for index, (first_leg, second_leg) in enumerate(LEGS[slot]):
+        for index, (first_leg, second_leg) in enumerate(legs_of(slot)):
             target = at_offset(first_leg[0] + second_leg[0], first_leg[1] + second_leg[1])
             pltpu.make_async_remote_copy(
                 src_ref=direction.at[slot, strip_rows(target)],
@@ -339,7 +331,7 @@
             ).start()
 
     for slot in range(slots):
-        for index, (first_leg, second_leg) in enumerate(LEGS[slot]):
+        for index, (first_leg, second_leg) in enumerate(legs_of(slot)):
             origin = at_offset(-first_leg[0], -first_leg[1])
             arrived(relayed.at[slot, index], relay_recv.at[slot, index])
             pltpu.make_async_remote_copy(
@@ -486,7 +478,7 @@
             vmem(right.shape, F32),
             vmem((slots, rows, columns), BF16),
             vmem((ranks, slots, strip, columns), BF16),
-            vmem((slots, len(LEGS[0]), strip, columns), BF16),
+            vmem((slots, len(LEGS), strip, columns), BF16),
             vmem((4, 8, 128), F32),
             vmem((ranks, 4, 8, 128), F32),
             vmem((per_group, 8, 128), F32),
@@ -505,7 +497,7 @@
             dma((slots,)),
             dma((slots,)),
             dma((slots,)),
-            dma((slots, len(LEGS[0]))),
+            dma((slots, len(LEGS))),
             dma,
             dma,
         ],

time: 60.1 us -> 60 us (level)
  no operation moved by 1% of the time
where the time goes in v2:
time: 60 us; the launch traced here: 59.8 us
  Pallas kernels  59.1 us (98%)
  between operations  0.64 us (1%)
    pallas_call x1, Pallas kernels, exchange(): pl.pallas_call(exchange_kernel, out_shape=(jax.ShapeDtypeStruct(first.sha...  56.2 us
    pallas_call x1, Pallas kernels, publish(): pl.pallas_call(publish_kernel, out_shape=[jax.ShapeDtypeStruct(value.shap...  2.92 us

profile of v2, /device:TPU:0, one launch (start us, length us, event | category | flops | bytes accessed | tf_op | source)
XLA Modules:
  0.0 59.8 jit_solution(3703632331338940884)
XLA Ops:
  0.6 56.2 %exchange.1 = (bf16[16,32,512]{2,1,0:T(8,128)(2,1)S(1)}, f32[16,32,512]{2,1,0:T(8,128)S(1)}, f32[16,32,512]{2,1,0:T(8,128)S(1)}, f32[2,512,512]{2,1,0:T(8,128)S(1)}, f32[2,512,512]{2,1,0:T(8,128)S(1)}) custom-call(s32[1,128]{1,0:T(1,128)} %bitcast.3, bf16[4,2,16,32,512]{4,3,2,1,0:T(8,128)(2,1)} %bitcast.2, bf16[2,512,512]{2,1,0:T(8,128)(2,1)} %root_left_ref.1, ...), custom_call_target="tpu_custom_call" | custom-call | flops 2147483648 | bytes 18874368 | tf_op jit(solution)/shard_map/exchange/pallas_call | solution.py:448
  56.9 2.9 %publish.1 = (bf16[16,32,512]{2,1,0:T(8,128)(2,1)}, f32[16,32,512]{2,1,0:T(8,128)}, f32[16,32,512]{2,1,0:T(8,128)}, f32[2,512,512]{2,1,0:T(8,128)}, f32[2,512,512]{2,1,0:T(8,128)}) custom-call(bf16[16,32,512]{2,1,0:T(8,128)(2,1)S(1)} %get-tuple-element.10.refs_0_, f32[16,32,512]{2,1,0:T(8,128)S(1)} %get-tuple-element.11.refs_1_, ...), custom_call_target="tpu_custom_call" | custom-call | tf_op jit(solution)/shard_map/publish/pallas_call | solution.py:542

commit v3 on v2

--- a/solution.py
+++ b/solution.py
@@ -11,6 +11,7 @@
 BF16 = jnp.bfloat16
 I32 = jnp.int32
 CHUNKS = 4
+GROUPS = ((0, 1), (2,), (3,))
 SIDE = 4
 NEAR = ((1, 0), (-1, 0), (0, 1), (0, -1), (1, 1), (-1, -1), (1, -1), (-1, 1))
 LEGS = (
@@ -54,7 +55,9 @@
     from_left,
     from_right,
     reduced,
-    outgoing,
+    outgoing_a,
+    outgoing_b,
+    outgoing_c,
     block,
     root_left,
     root_right,
@@ -70,6 +73,7 @@
     sizes,
     graft,
     update,
+    adam_sums,
     place_sem,
     own_sem,
     load_sem,
@@ -87,8 +91,9 @@
     sums_send,
     sums_recv,
 ):
+    outgoing = (outgoing_a, outgoing_b, outgoing_c)
     lines, _, per_group, strip, columns = grad_ref.shape
-    width = columns // CHUNKS
+    height, width = strip // 2, columns // 2
     half = per_group // 2
     slots, rows = block.shape[:2]
     ranks = rows // strip
@@ -108,8 +113,11 @@
     left = behind * 2 + core
     chunks = range(CHUNKS)
 
+    def upper(k):
+        return pl.ds(k // 2 * height, height)
+
     def cols(k):
-        return pl.ds(k * width, width)
+        return pl.ds(k % 2 * width, width)
 
     def strip_rows(at):
         return pl.ds(pl.multiple_of(at * strip, strip), strip)
@@ -132,13 +140,18 @@
 
     owner_load = pltpu.make_async_copy(owner_ref, owner, place_sem.at[0])
     owner_load.start()
-    own_loads = []
-    for k in chunks:
-        load = pltpu.make_async_copy(
-            grad_ref.at[:, core, :, :, cols(k)], own.at[k], own_sem.at[k]
-        )
-        load.start()
-        own_loads.append(load)
+    order = (across, ahead, behind, x)
+    own_loads = {}
+    for part in range(2):
+        for index, line in enumerate(order):
+            there = pl.ds(part * height, height)
+            load = pltpu.make_async_copy(
+                grad_ref.at[line, core, :, there],
+                own.at[line, :, there],
+                own_sem.at[part, index],
+            )
+            load.start()
+            own_loads[part, index] = load
     loads = [
         pltpu.make_async_copy(src, dst, load_sem.at[index])
         for index, (src, dst) in enumerate(
@@ -183,20 +196,19 @@
 
     pl.semaphore_wait(barrier, ranks + 2)
 
-    core_copies = []
-    for k in chunks:
-        copies = []
-        for index, line in enumerate((across, ahead, behind, x)):
+    core_copies = {}
+    for part in range(2):
+        for index, line in enumerate(order):
+            there = pl.ds(part * height, height)
             copy = pltpu.make_async_remote_copy(
-                src_ref=grad_ref.at[line, 1 - core, :, :, cols(k)],
-                dst_ref=other.at[k, line],
-                send_sem=core_send.at[k, index],
-                recv_sem=core_recv.at[k, line],
+                src_ref=grad_ref.at[line, 1 - core, :, there],
+                dst_ref=other.at[line, :, there],
+                send_sem=core_send.at[part, index],
+                recv_sem=core_recv.at[part, line],
                 device_id={"dp": mate},
             )
             copy.start()
-            copies.append(copy)
-        core_copies.append(copies)
+            core_copies[part, index] = copy
     place_copy.wait()
 
     def held(at):
@@ -208,9 +220,21 @@
     def place_of(index):
         return jnp.clip(place[0, dp * per_group + index], 0, ranks * slots - 1)
 
-    def wait_core(k, line):
-        ref = other.at[k, line]
-        pltpu.make_async_copy(ref, ref, core_recv.at[k, line]).wait()
+    def ready(k, index):
+        if k % 2 == 0:
+            part, line = k // 2, order[index]
+            own_loads[part, index].wait()
+            ref = other.at[line, :, upper(k)]
+            pltpu.make_async_copy(ref, ref, core_recv.at[part, line]).wait()
+
+    def both(k, index):
+        line = order[index]
+        return own[line, :, upper(k), cols(k)], other[line, :, upper(k), cols(k)]
+
+    def pair_sum(k, index):
+        ready(k, index)
+        mine, its = both(k, index)
+        pair[k, order[index]] = mine + its
 
     def ring(k, index, src, dst, target):
         return pltpu.make_async_remote_copy(
@@ -234,19 +258,15 @@
             ring(k, 5, pair.at[k, behind, high], from_right.at[k, high], left),
         ]
         ring_copies[k] = copies
-        own_loads[k].wait()
-        wait_core(k, across)
-        pair[k, across] = own[k, across] + other[k, across]
+        pair_sum(k, 0)
         copies[0].start()
         copies[1].start()
 
     def near_sums(k):
         copies = ring_copies[k]
-        wait_core(k, ahead)
-        pair[k, ahead] = own[k, ahead] + other[k, ahead]
+        pair_sum(k, 1)
         copies[2].start()
-        wait_core(k, behind)
-        pair[k, behind] = own[k, behind] + other[k, behind]
+        pair_sum(k, 2)
         copies[3].start()
 
     def relay(k):
@@ -258,27 +278,56 @@
         pair[k, behind, high] = pair[k, behind, high] + relay_left[k]
         copies[5].start()
     def finish(k):
-        wait_core(k, x)
-        total = own[k, x].astype(F32) + other[k, x].astype(F32)
+        ready(k, 3)
+        mine, its = both(k, 3)
+        total = mine.astype(F32) + its.astype(F32)
         for copy in ring_copies[k][2:]:
             copy.wait_recv()
         total = total + from_left[k].astype(F32) + from_right[k].astype(F32)
         reduced[k] = total.astype(BF16)
 
+    def group_rows(group):
+        return pl.ds(
+            pl.multiple_of(rank * strip + GROUPS[group][0] // 2 * height, height), height
+        )
+
+    def group_cols(group):
+        return pl.ds(GROUPS[group][0] % 2 * width, len(GROUPS[group]) * width)
+
+    def to_owners(group):
         def visit(target):
             for slot in range(slots):
-                outgoing[k, target, slot] = reduced[k, block_of(target * slots + slot)]
+                at = block_of(target * slots + slot)
+                for index, k in enumerate(GROUPS[group]):
+                    outgoing[group][target, slot, :, cols(index)] = reduced[k, at]
             pltpu.make_async_remote_copy(
-                src_ref=outgoing.at[k, target],
-                dst_ref=block.at[:, strip_rows(rank), cols(k)],
-                send_sem=owner_send.at[k],
-                recv_sem=owner_recv.at[k],
+                src_ref=outgoing[group].at[target],
+                dst_ref=block.at[:, group_rows(group), group_cols(group)],
+                send_sem=owner_send.at[group],
+                recv_sem=owner_recv.at[group],
                 device_id={"fsdp": target},
             ).start()
 
         each_target(visit)
         for slot in range(slots):
-            block[slot, strip_rows(rank), cols(k)] = reduced[k, block_of(rank * slots + slot)]
+            at = block_of(rank * slots + slot)
+            for k in GROUPS[group]:
+                block[slot, group_rows(group), cols(k)] = reduced[k, at]
+
+    def moments(k):
+        step = 4
+
+        @pl.loop(0, per_group // step)
+        def _(turn):
+            here = pl.ds(turn * step, step)
+            grad = reduced[k, here].astype(F32)
+            first_new = 0.9 * first[here, upper(k), cols(k)] + 0.1 * grad
+            second_new = 0.95 * second[here, upper(k), cols(k)] + 0.05 * grad * grad
+            first[here, upper(k), cols(k)] = first_new
+            second[here, upper(k), cols(k)] = second_new
+            adam = first_new / (jnp.sqrt(second_new) + 1e-08)
+            adam = jnp.sum((adam * adam).reshape(step, height // 8, 8, width), axis=1)
+            adam_sums[k, here] = adam[:, :, :128] + adam[:, :, 128:]
 
     far_sums(0)
     near_sums(0)
@@ -286,22 +335,42 @@
     relay(0)
     for load in loads:
         load.start()
-    for k in chunks:
-        if k + 1 < CHUNKS:
-            near_sums(k + 1)
-        if k + 2 < CHUNKS:
-            far_sums(k + 2)
-        if k + 1 < CHUNKS:
-            relay(k + 1)
-        finish(k)
+    near_sums(1)
+    far_sums(2)
+    relay(1)
+    finish(0)
+    loads[2].wait()
+    loads[3].wait()
+    near_sums(2)
+    far_sums(3)
+    moments(0)
+    relay(2)
+    finish(1)
+    to_owners(0)
+    near_sums(3)
+    relay(3)
+    moments(1)
+    finish(2)
+    to_owners(1)
+    finish(3)
+    to_owners(2)
+    moments(2)
+    moments(3)
+
+    stores = [
+        pltpu.make_async_copy(first, first_out, store_sem.at[0]),
+        pltpu.make_async_copy(second, second_out, store_sem.at[1]),
+    ]
+    for store in stores:
+        store.start()
 
     others = (ranks - 1) * strip
 
     def arrived(ref, sem):
         pltpu.make_async_copy(ref, ref, sem).wait()
 
-    for k in chunks:
-        arrived(block.at[:, pl.ds(0, others), cols(k)], owner_recv.at[k])
+    for group in range(len(GROUPS)):
+        arrived(outgoing[group].at[pl.ds(0, ranks - 1)], owner_recv.at[group])
     loads[0].wait()
     loads[1].wait()
 
@@ -349,23 +418,9 @@
         sums[2 + slot] = functools.reduce(
             jnp.add, [wide[:, at : at + 128] for at in range(0, columns, 128)]
         )
-    loads[2].wait()
-    loads[3].wait()
-
-    @pl.loop(0, per_group)
-    def _(index):
-        total = jnp.zeros((1, 128), F32)
-        for k in chunks:
-            grad = reduced[k, index].astype(F32)
-            first_new = 0.9 * first[index, :, cols(k)] + 0.1 * grad
-            second_new = 0.95 * second[index, :, cols(k)] + 0.05 * grad * grad
-            first[index, :, cols(k)] = first_new
-            second[index, :, cols(k)] = second_new
-            adam = first_new / (jnp.sqrt(second_new) + 1e-08)
-            part = jnp.sum(adam * adam, axis=0, keepdims=True)
-            for at in range(0, width, 128):
-                total = total + part[:, at : at + 128]
-        sums[index // 8, pl.ds(index % 8, 1)] = total
+    adam = jnp.sum(jnp.sum(adam_sums[...], axis=0), axis=1)
+    for index in range(2):
+        sums[index] = adam[index * 8 : index * 8 + 8]
 
     def send_sums(target):
         pltpu.make_async_remote_copy(
@@ -378,13 +433,6 @@
 
     each_target(send_sums)
     all_sums[rank] = sums[...]
-    stores = [
-        pltpu.make_async_copy(first, first_out, store_sem.at[0]),
-        pltpu.make_async_copy(second, second_out, store_sem.at[1]),
-    ]
-    for store in stores:
-        store.start()
-
     loads[4].wait()
     loads[5].wait()
     for stat, contract, index, out in ((stat_left, 1, 2, left_out), (stat_right, 0, 3, right_out)):
@@ -425,9 +473,12 @@
     stores.append(store)
 
     for k in chunks:
-        for copy in core_copies[k] + ring_copies[k]:
+        for copy in ring_copies[k]:
             copy.wait_send()
-        arrived(outgoing.at[k, pl.ds(0, ranks - 1)], owner_send.at[k])
+    for copy in core_copies.values():
+        copy.wait_send()
+    for group in range(len(GROUPS)):
+        arrived(outgoing[group].at[pl.ds(0, ranks - 1)], owner_send.at[group])
     for slot in range(slots):
         arrived(direction.at[slot, pl.ds(0, others)], back_send.at[slot])
         arrived(relayed.at[slot], relay_send.at[slot])
@@ -439,7 +490,7 @@
 def exchange(block_owner, gradients, root_left, root_right, first, second, left, right, ranks):
     lines, _, per_group, strip, columns = gradients.shape
     slots, rows, _ = root_left.shape
-    width = columns // CHUNKS
+    height, width = strip // 2, columns // 2
     half = per_group // 2
     anywhere = pl.BlockSpec(memory_space=pl.ANY)
     far = pl.BlockSpec(memory_space=pltpu.HBM)
@@ -460,15 +511,18 @@
             vmem(block_owner.shape, I32),
             vmem((8, 128), I32),
             pltpu.SMEM((8, 128), I32),
-            vmem((CHUNKS, lines, per_group, strip, width), BF16),
-            vmem((CHUNKS, lines, per_group, strip, width), BF16),
-            vmem((CHUNKS, lines, per_group, strip, width), BF16),
-            vmem((CHUNKS, half, strip, width), BF16),
-            vmem((CHUNKS, half, strip, width), BF16),
-            vmem((CHUNKS, per_group, strip, width), BF16),
-            vmem((CHUNKS, per_group, strip, width), BF16),
-            vmem((CHUNKS, per_group, strip, width), BF16),
-            vmem((CHUNKS, ranks, slots, strip, width), BF16),
+            vmem((lines, per_group, strip, columns), BF16),
+            vmem((lines, per_group, strip, columns), BF16),
+            vmem((CHUNKS, lines, per_group, height, width), BF16),
+            vmem((CHUNKS, half, height, width), BF16),
+            vmem((CHUNKS, half, height, width), BF16),
+            vmem((CHUNKS, per_group, height, width), BF16),
+            vmem((CHUNKS, per_group, height, width), BF16),
+            vmem((CHUNKS, per_group, height, width), BF16),
+            *(
+                vmem((ranks, slots, height, len(group) * width), BF16)
+                for group in GROUPS
+            ),
             vmem((slots, rows, columns), BF16),
             vmem((slots, rows, columns), BF16),
             vmem((slots, rows, columns), BF16),
@@ -484,16 +538,17 @@
             vmem((per_group, 8, 128), F32),
             vmem((per_group, 128), F32),
             vmem((per_group, strip, columns), BF16),
+            vmem((CHUNKS, per_group, 8, 128), F32),
             dma((2,)),
-            dma((CHUNKS,)),
+            dma((2, 4)),
             dma((6,)),
             dma((5,)),
-            dma((CHUNKS, 4)),
-            dma((CHUNKS, 4)),
+            dma((2, 4)),
+            dma((2, 4)),
             dma((CHUNKS, 6)),
             dma((CHUNKS, 6)),
-            dma((CHUNKS,)),
-            dma((CHUNKS,)),
+            dma((len(GROUPS),)),
+            dma((len(GROUPS),)),
             dma((slots,)),
             dma((slots,)),
             dma((slots,)),

time: 60 us -> 61.6 us (1.027)
  Pallas kernels: 59.1 us -> 60.7 us
    pallas_call x1, Pallas kernels: 56.2 us -> 57.7 us  [exchange(): pl.pallas_call(exchange_kernel, out_shape=(jax.ShapeDtypeStruct(first.sha...]
where the time goes in v3:
time: 61.6 us; the launch traced here: 61.3 us
  Pallas kernels  60.7 us (99%)
  between operations  0.64 us (1%)
    pallas_call x1, Pallas kernels, exchange(): pl.pallas_call(exchange_kernel, out_shape=(jax.ShapeDtypeStruct(first.sha...  57.7 us
    pallas_call x1, Pallas kernels, publish(): pl.pallas_call(publish_kernel, out_shape=[jax.ShapeDtypeStruct(value.shap...  2.92 us

profile of v3, /device:TPU:0, one launch (start us, length us, event | category | flops | bytes accessed | tf_op | source)
XLA Modules:
  0.0 61.3 jit_solution(9979291137851941889)
XLA Ops:
  0.6 57.7 %exchange.1 = (bf16[16,32,512]{2,1,0:T(8,128)(2,1)S(1)}, f32[16,32,512]{2,1,0:T(8,128)S(1)}, f32[16,32,512]{2,1,0:T(8,128)S(1)}, f32[2,512,512]{2,1,0:T(8,128)S(1)}, f32[2,512,512]{2,1,0:T(8,128)S(1)}) custom-call(s32[1,128]{1,0:T(1,128)} %bitcast.3, bf16[4,2,16,32,512]{4,3,2,1,0:T(8,128)(2,1)} %bitcast.2, bf16[2,512,512]{2,1,0:T(8,128)(2,1)} %root_left_ref.1, ...), custom_call_target="tpu_custom_call" | custom-call | flops 2147483648 | bytes 18874368 | tf_op jit(solution)/shard_map/exchange/pallas_call | solution.py:499
  58.4 2.9 %publish.1 = (bf16[16,32,512]{2,1,0:T(8,128)(2,1)}, f32[16,32,512]{2,1,0:T(8,128)}, f32[16,32,512]{2,1,0:T(8,128)}, f32[2,512,512]{2,1,0:T(8,128)}, f32[2,512,512]{2,1,0:T(8,128)}) custom-call(bf16[16,32,512]{2,1,0:T(8,128)(2,1)S(1)} %get-tuple-element.10.refs_0_, f32[16,32,512]{2,1,0:T(8,128)S(1)} %get-tuple-element.11.refs_1_, ...), custom_call_target="tpu_custom_call" | custom-call | tf_op jit(solution)/shard_map/publish/pallas_call | solution.py:597

commit v4 on v3

--- a/solution.py
+++ b/solution.py
@@ -10,8 +10,8 @@
 F32 = jnp.float32
 BF16 = jnp.bfloat16
 I32 = jnp.int32
-CHUNKS = 4
-GROUPS = ((0, 1), (2,), (3,))
+PARTS = ((0, 0, 1), (0, 1, 1), (0, 2, 2), (1, 0, 2), (1, 2, 1), (1, 3, 1))
+CHUNKS = len(PARTS)
 SIDE = 4
 NEAR = ((1, 0), (-1, 0), (0, 1), (0, -1), (1, 1), (-1, -1), (1, -1), (-1, 1))
 LEGS = (
@@ -39,7 +39,9 @@
     second_ref,
     left_ref,
     right_ref,
-    update_out,
+    returned,
+    graft_out,
+    places_out,
     first_out,
     second_out,
     left_out,
@@ -55,9 +57,7 @@
     from_left,
     from_right,
     reduced,
-    outgoing_a,
-    outgoing_b,
-    outgoing_c,
+    outgoing,
     block,
     root_left,
     root_right,
@@ -66,13 +66,11 @@
     stat_left,
     stat_right,
     direction,
-    returned,
     relayed,
     sums,
     all_sums,
     sizes,
     graft,
-    update,
     adam_sums,
     place_sem,
     own_sem,
@@ -91,9 +89,8 @@
     sums_send,
     sums_recv,
 ):
-    outgoing = (outgoing_a, outgoing_b, outgoing_c)
     lines, _, per_group, strip, columns = grad_ref.shape
-    height, width = strip // 2, columns // 2
+    height = strip // 2
     half = per_group // 2
     slots, rows = block.shape[:2]
     ranks = rows // strip
@@ -114,10 +111,10 @@
     chunks = range(CHUNKS)
 
     def upper(k):
-        return pl.ds(k // 2 * height, height)
+        return pl.ds(PARTS[k][0] * height, height)
 
     def cols(k):
-        return pl.ds(k % 2 * width, width)
+        return pl.ds(PARTS[k][1] * 128, PARTS[k][2] * 128)
 
     def strip_rows(at):
         return pl.ds(pl.multiple_of(at * strip, strip), strip)
@@ -221,8 +218,8 @@
         return jnp.clip(place[0, dp * per_group + index], 0, ranks * slots - 1)
 
     def ready(k, index):
-        if k % 2 == 0:
-            part, line = k // 2, order[index]
+        if PARTS[k][1] == 0:
+            part, line = PARTS[k][0], order[index]
             own_loads[part, index].wait()
             ref = other.at[line, :, upper(k)]
             pltpu.make_async_copy(ref, ref, core_recv.at[part, line]).wait()
@@ -234,7 +231,7 @@
     def pair_sum(k, index):
         ready(k, index)
         mine, its = both(k, index)
-        pair[k, order[index]] = mine + its
+        pair[k][order[index]] = mine + its
 
     def ring(k, index, src, dst, target):
         return pltpu.make_async_remote_copy(
@@ -250,12 +247,12 @@
 
     def far_sums(k):
         copies = [
-            ring(k, 0, pair.at[k, across, low], relay_right.at[k], right),
-            ring(k, 1, pair.at[k, across, high], relay_left.at[k], left),
-            ring(k, 2, pair.at[k, ahead, high], from_left.at[k, high], right),
-            ring(k, 3, pair.at[k, behind, low], from_right.at[k, low], left),
-            ring(k, 4, pair.at[k, ahead, low], from_left.at[k, low], right),
-            ring(k, 5, pair.at[k, behind, high], from_right.at[k, high], left),
+            ring(k, 0, pair[k].at[across, low], relay_right[k], right),
+            ring(k, 1, pair[k].at[across, high], relay_left[k], left),
+            ring(k, 2, pair[k].at[ahead, high], from_left[k].at[high], right),
+            ring(k, 3, pair[k].at[behind, low], from_right[k].at[low], left),
+            ring(k, 4, pair[k].at[ahead, low], from_left[k].at[low], right),
+            ring(k, 5, pair[k].at[behind, high], from_right[k].at[high], left),
         ]
         ring_copies[k] = copies
         pair_sum(k, 0)
@@ -272,10 +269,10 @@
     def relay(k):
         copies = ring_copies[k]
         copies[0].wait_recv()
-        pair[k, ahead, low] = pair[k, ahead, low] + relay_right[k]
+        pair[k][ahead, low] = pair[k][ahead, low] + relay_right[k][...]
         copies[4].start()
         copies[1].wait_recv()
-        pair[k, behind, high] = pair[k, behind, high] + relay_left[k]
+        pair[k][behind, high] = pair[k][behind, high] + relay_left[k][...]
         copies[5].start()
     def finish(k):
         ready(k, 3)
@@ -283,36 +280,27 @@
         total = mine.astype(F32) + its.astype(F32)
         for copy in ring_copies[k][2:]:
             copy.wait_recv()
-        total = total + from_left[k].astype(F32) + from_right[k].astype(F32)
-        reduced[k] = total.astype(BF16)
-
-    def group_rows(group):
-        return pl.ds(
-            pl.multiple_of(rank * strip + GROUPS[group][0] // 2 * height, height), height
-        )
-
-    def group_cols(group):
-        return pl.ds(GROUPS[group][0] % 2 * width, len(GROUPS[group]) * width)
-
-    def to_owners(group):
+        total = total + from_left[k][...].astype(F32) + from_right[k][...].astype(F32)
+        reduced[k][...] = total.astype(BF16)
+
+    def strip_part(k):
+        return pl.ds(pl.multiple_of(rank * strip + PARTS[k][0] * height, height), height)
+
+    def to_owners(k):
         def visit(target):
             for slot in range(slots):
-                at = block_of(target * slots + slot)
-                for index, k in enumerate(GROUPS[group]):
-                    outgoing[group][target, slot, :, cols(index)] = reduced[k, at]
+                outgoing[k][target, slot] = reduced[k][block_of(target * slots + slot)]
             pltpu.make_async_remote_copy(
-                src_ref=outgoing[group].at[target],
-                dst_ref=block.at[:, group_rows(group), group_cols(group)],
-                send_sem=owner_send.at[group],
-                recv_sem=owner_recv.at[group],
+                src_ref=outgoing[k].at[target],
+                dst_ref=block.at[:, strip_part(k), cols(k)],
+                send_sem=owner_send.at[k],
+                recv_sem=owner_recv.at[k],
                 device_id={"fsdp": target},
             ).start()
 
         each_target(visit)
         for slot in range(slots):
-            at = block_of(rank * slots + slot)
-            for k in GROUPS[group]:
-                block[slot, group_rows(group), cols(k)] = reduced[k, at]
+            block[slot, strip_part(k), cols(k)] = reduced[k][block_of(rank * slots + slot)]
 
     def moments(k):
         step = 4
@@ -320,14 +308,16 @@
         @pl.loop(0, per_group // step)
         def _(turn):
             here = pl.ds(turn * step, step)
-            grad = reduced[k, here].astype(F32)
+            grad = reduced[k][here].astype(F32)
             first_new = 0.9 * first[here, upper(k), cols(k)] + 0.1 * grad
             second_new = 0.95 * second[here, upper(k), cols(k)] + 0.05 * grad * grad
             first[here, upper(k), cols(k)] = first_new
             second[here, upper(k), cols(k)] = second_new
             adam = first_new / (jnp.sqrt(second_new) + 1e-08)
-            adam = jnp.sum((adam * adam).reshape(step, height // 8, 8, width), axis=1)
-            adam_sums[k, here] = adam[:, :, :128] + adam[:, :, 128:]
+            adam = jnp.sum((adam * adam).reshape(step, height // 8, 8, -1), axis=1)
+            adam_sums[k, here] = functools.reduce(
+                jnp.add, [adam[:, :, at * 128 : at * 128 + 128] for at in range(PARTS[k][2])]
+            )
 
     far_sums(0)
     near_sums(0)
@@ -335,27 +325,22 @@
     relay(0)
     for load in loads:
         load.start()
-    near_sums(1)
-    far_sums(2)
-    relay(1)
-    finish(0)
-    loads[2].wait()
-    loads[3].wait()
-    near_sums(2)
-    far_sums(3)
-    moments(0)
-    relay(2)
-    finish(1)
-    to_owners(0)
-    near_sums(3)
-    relay(3)
-    moments(1)
-    finish(2)
-    to_owners(1)
-    finish(3)
-    to_owners(2)
-    moments(2)
-    moments(3)
+    for k in chunks:
+        if k + 1 < CHUNKS:
+            near_sums(k + 1)
+        if k + 2 < CHUNKS:
+            far_sums(k + 2)
+        if k + 1 < CHUNKS:
+            relay(k + 1)
+        if k == 1:
+            loads[2].wait()
+            loads[3].wait()
+        if 1 <= k < CHUNKS - 2:
+            moments(k - 1)
+        finish(k)
+        to_owners(k)
+    for k in range(CHUNKS - 3, CHUNKS):
+        moments(k)
 
     stores = [
         pltpu.make_async_copy(first, first_out, store_sem.at[0]),
@@ -369,8 +354,8 @@
     def arrived(ref, sem):
         pltpu.make_async_copy(ref, ref, sem).wait()
 
-    for group in range(len(GROUPS)):
-        arrived(outgoing[group].at[pl.ds(0, ranks - 1)], owner_recv.at[group])
+    for k in chunks:
+        arrived(outgoing[k].at[pl.ds(0, ranks - 1)], owner_recv.at[k])
     loads[0].wait()
     loads[1].wait()
 
@@ -412,7 +397,11 @@
             ).start()
 
     for slot in range(slots):
-        returned[rank, slot] = direction[slot, strip_rows(rank)]
+        keep = pltpu.make_async_copy(
+            direction.at[slot, strip_rows(rank)], returned.at[rank, slot], store_sem.at[4 + slot]
+        )
+        keep.start()
+        stores.append(keep)
         wide = direction[slot].astype(F32)
         wide = jnp.sum((wide * wide).reshape(-1, 8, columns), axis=0)
         sums[2 + slot] = functools.reduce(
@@ -458,27 +447,20 @@
     direction_sq = jnp.sum(jnp.sum(sizes[...], axis=1), axis=1, keepdims=True)
     graft[...] = jnp.broadcast_to(jnp.sqrt(adam_sq / (direction_sq + 1e-06)), graft.shape)
 
+    for index, (src, out) in enumerate(((graft, graft_out), (places, places_out))):
+        store = pltpu.make_async_copy(src, out, store_sem.at[6 + index])
+        store.start()
+        stores.append(store)
     for slot in range(slots):
         arrived(returned.at[pl.ds(0, ranks - 1), slot], back_recv.at[slot])
-
-    @pl.loop(0, per_group)
-    def _(index):
-        at = place_of(index)
-        scale = -graft[pl.ds(index, 1)]
-        value = returned[at // slots, at % slots].astype(F32)
-        update[index] = (value * jnp.concatenate([scale] * (columns // 128), axis=1)).astype(BF16)
-
-    store = pltpu.make_async_copy(update, update_out, store_sem.at[4])
-    store.start()
-    stores.append(store)
 
     for k in chunks:
         for copy in ring_copies[k]:
             copy.wait_send()
     for copy in core_copies.values():
         copy.wait_send()
-    for group in range(len(GROUPS)):
-        arrived(outgoing[group].at[pl.ds(0, ranks - 1)], owner_send.at[group])
+    for k in chunks:
+        arrived(outgoing[k].at[pl.ds(0, ranks - 1)], owner_send.at[k])
     for slot in range(slots):
         arrived(direction.at[slot, pl.ds(0, others)], back_send.at[slot])
         arrived(relayed.at[slot], relay_send.at[slot])
@@ -490,7 +472,8 @@
 def exchange(block_owner, gradients, root_left, root_right, first, second, left, right, ranks):
     lines, _, per_group, strip, columns = gradients.shape
     slots, rows, _ = root_left.shape
-    height, width = strip // 2, columns // 2
+    height = strip // 2
+    widths = [tiles * 128 for _, _, tiles in PARTS]
     half = per_group // 2
     anywhere = pl.BlockSpec(memory_space=pl.ANY)
     far = pl.BlockSpec(memory_space=pltpu.HBM)
@@ -499,30 +482,29 @@
     return pl.pallas_call(
         exchange_kernel,
         out_shape=(
-            jax.ShapeDtypeStruct(first.shape, BF16),
+            jax.ShapeDtypeStruct((ranks, slots, strip, columns), BF16),
+            jax.ShapeDtypeStruct((per_group, 128), F32),
+            jax.ShapeDtypeStruct((8, 128), I32),
             jax.ShapeDtypeStruct(first.shape, F32),
             jax.ShapeDtypeStruct(first.shape, F32),
             jax.ShapeDtypeStruct(left.shape, F32),
             jax.ShapeDtypeStruct(right.shape, F32),
         ),
         in_specs=[far] * 8,
-        out_specs=(anywhere,) * 5,
+        out_specs=(anywhere,) * 7,
         scratch_shapes=[
             vmem(block_owner.shape, I32),
             vmem((8, 128), I32),
             pltpu.SMEM((8, 128), I32),
             vmem((lines, per_group, strip, columns), BF16),
             vmem((lines, per_group, strip, columns), BF16),
-            vmem((CHUNKS, lines, per_group, height, width), BF16),
-            vmem((CHUNKS, half, height, width), BF16),
-            vmem((CHUNKS, half, height, width), BF16),
-            vmem((CHUNKS, per_group, height, width), BF16),
-            vmem((CHUNKS, per_group, height, width), BF16),
-            vmem((CHUNKS, per_group, height, width), BF16),
-            *(
-                vmem((ranks, slots, height, len(group) * width), BF16)
-                for group in GROUPS
-            ),
+            [vmem((lines, per_group, height, wide), BF16) for wide in widths],
+            [vmem((half, height, wide), BF16) for wide in widths],
+            [vmem((half, height, wide), BF16) for wide in widths],
+            [vmem((per_group, height, wide), BF16) for wide in widths],
+            [vmem((per_group, height, wide), BF16) for wide in widths],
+            [vmem((per_group, height, wide), BF16) for wide in widths],
+            [vmem((ranks, slots, height, wide), BF16) for wide in widths],
             vmem((slots, rows, columns), BF16),
             vmem((slots, rows, columns), BF16),
             vmem((slots, rows, columns), BF16),
@@ -531,24 +513,22 @@
             vmem(left.shape, F32),
             vmem(right.shape, F32),
             vmem((slots, rows, columns), BF16),
-            vmem((ranks, slots, strip, columns), BF16),
             vmem((slots, len(LEGS), strip, columns), BF16),
             vmem((4, 8, 128), F32),
             vmem((ranks, 4, 8, 128), F32),
             vmem((per_group, 8, 128), F32),
             vmem((per_group, 128), F32),
-            vmem((per_group, strip, columns), BF16),
             vmem((CHUNKS, per_group, 8, 128), F32),
             dma((2,)),
             dma((2, 4)),
             dma((6,)),
-            dma((5,)),
+            dma((8,)),
             dma((2, 4)),
             dma((2, 4)),
             dma((CHUNKS, 6)),
             dma((CHUNKS, 6)),
-            dma((len(GROUPS),)),
-            dma((len(GROUPS),)),
+            dma((CHUNKS,)),
+            dma((CHUNKS,)),
             dma((slots,)),
             dma((slots,)),
             dma((slots,)),
@@ -580,27 +560,65 @@
     )
 
 
-def publish_kernel(*refs):
-    count = (len(refs) - 1) // 2
-    sems = refs[-1]
+def publish_kernel(
+    returned,
+    graft,
+    places,
+    first,
+    second,
+    left,
+    right,
+    update_out,
+    first_out,
+    second_out,
+    left_out,
+    right_out,
+    place,
+    update,
+    sems,
+):
+    per_group, strip, columns = update.shape
+    ranks, slots = returned.shape[:2]
+    place_copy = pltpu.make_async_copy(places, place, sems.at[5])
+    place_copy.start()
+    pairs = ((left, left_out), (right, right_out), (first, first_out), (second, second_out))
     copies = [
-        pltpu.make_async_copy(refs[index], refs[count + index], sems.at[index])
-        for index in range(count)
+        pltpu.make_async_copy(src, out, sems.at[index]) for index, (src, out) in enumerate(pairs)
     ]
     for copy in copies:
         copy.start()
+    place_copy.wait()
+    dp = lax.axis_index("dp")
+
+    @pl.loop(0, per_group)
+    def _(index):
+        at = jnp.clip(place[0, dp * per_group + index], 0, ranks * slots - 1)
+        scale = -graft[pl.ds(index, 1)]
+        value = returned[at // slots, at % slots].astype(F32)
+        update[index] = (value * jnp.concatenate([scale] * (columns // 128), axis=1)).astype(BF16)
+
+    copies.append(pltpu.make_async_copy(update, update_out, sems.at[4]))
+    copies[-1].start()
     for copy in copies:
         copy.wait()
 
 
 def publish(results):
+    returned, graft, places, first, second, left, right = results
+    anywhere = pl.BlockSpec(memory_space=pl.ANY)
+    near = pl.BlockSpec(memory_space=pltpu.VMEM)
+    shapes = [(first.shape, BF16)] + [(value.shape, F32) for value in results[3:]]
     return pl.pallas_call(
         publish_kernel,
-        out_shape=[jax.ShapeDtypeStruct(value.shape, value.dtype) for value in results],
-        in_specs=[pl.BlockSpec(memory_space=pl.ANY)] * len(results),
-        out_specs=[pl.BlockSpec(memory_space=pltpu.HBM)] * len(results),
-        scratch_shapes=[pltpu.SemaphoreType.DMA((len(results),))],
-        compiler_params=pltpu.CompilerParams(vmem_limit_bytes=2**20),
+        out_shape=[jax.ShapeDtypeStruct(*shape) for shape in shapes],
+        in_specs=[near, near] + [anywhere] * 5,
+        out_specs=[pl.BlockSpec(memory_space=pltpu.HBM)] * 5,
+        scratch_shapes=[
+            pltpu.SMEM((8, 128), I32),
+            pltpu.VMEM(first.shape, BF16),
+            pltpu.SemaphoreType.DMA((6,)),
+        ],
+        compiler_params=pltpu.CompilerParams(vmem_limit_bytes=4 * 2**20),
         name="publish",
     )(*(pltpu.with_memory_space_constraint(value, pltpu.VMEM) for value in results))
 

time: 61.6 us -> 58.4 us (0.948)
  Pallas kernels: 60.7 us -> 57.6 us
    pallas_call x2, Pallas kernels: 60.7 us -> 57.6 us  [the longest x1 54.8 us: exchange(): pl.pallas_call(exchange_kernel, out_shape=(jax.ShapeDtypeStruct((ranks, s...]
where the time goes in v4:
time: 58.4 us; the launch traced here: 58.3 us
  Pallas kernels  57.6 us (99%)
  between operations  0.64 us (1%)
    pallas_call x1, Pallas kernels, exchange(): pl.pallas_call(exchange_kernel, out_shape=(jax.ShapeDtypeStruct((ranks, s...  54.8 us
    pallas_call x1, Pallas kernels, publish(): pl.pallas_call(publish_kernel, out_shape=[jax.ShapeDtypeStruct(*shape) fo...  2.86 us

profile of v4, /device:TPU:0, one launch (start us, length us, event | category | flops | bytes accessed | tf_op | source)
XLA Modules:
  0.0 58.3 jit_solution(5774348649011868491)
XLA Ops:
  0.6 54.8 %exchange.1 = (bf16[16,2,32,512]{3,2,1,0:T(8,128)(2,1)S(1)}, f32[16,128]{1,0:T(8,128)S(1)}, s32[8,128]{1,0:T(8,128)S(1)}, f32[16,32,512]{2,1,0:T(8,128)S(1)}, f3...) custom-call(s32[1,128]{1,0:T(1,128)} %bitcast.3, ...), custom_call_target="tpu_custom_call" | custom-call | flops 2147483648 | bytes 18874368 | tf_op jit(solution)/shard_map/exchange/pallas_call | solution.py:482
  55.4 2.9 %publish.1 = (bf16[16,32,512]{2,1,0:T(8,128)(2,1)}, f32[16,32,512]{2,1,0:T(8,128)}, f32[16,32,512]{2,1,0:T(8,128)}, f32[2,512,512]{2,1,0:T(8,128)}, f32[2,512,512]{2,1,0:T(8,128)}) custom-call(bf16[16,2,32,512]{3,2,1,0:T(8,128)(2,1)S(1)} %get-tuple-element.12.returned, f32[16,128]{1,0:T(8,128)S(1)} %get-tuple-element.13.graft, ...), custom_call_target="tpu_custom_call" | custom-call | tf_op jit(solution)/shard_map/publish/pallas_call | solution.py:611

commit v5 on v4

--- a/solution.py
+++ b/solution.py
@@ -13,7 +13,7 @@
 PARTS = ((0, 0, 1), (0, 1, 1), (0, 2, 2), (1, 0, 2), (1, 2, 1), (1, 3, 1))
 CHUNKS = len(PARTS)
 SIDE = 4
-NEAR = ((1, 0), (-1, 0), (0, 1), (0, -1), (1, 1), (-1, -1), (1, -1), (-1, 1))
+NEAR = ((1, 1), (-1, -1), (1, -1), (-1, 1), (1, 0), (-1, 0), (0, 1), (0, -1))
 LEGS = (
     ((1, 1), (1, 1)),
     ((-1, 1), (-1, 0)),
@@ -84,8 +84,10 @@
     owner_recv,
     back_send,
     back_recv,
+    leg_send,
     relay_send,
     relay_recv,
+    last_recv,
     sums_send,
     sums_recv,
 ):
@@ -124,8 +126,8 @@
         target_z = (z + SIDE + sign * dz) % SIDE
         return target_z * SIDE + target_y
 
-    def each_target(visit):
-        @pl.loop(0, SIDE)
+    def each_target(visit, turns=(0, SIDE)):
+        @pl.loop(*turns)
         def _(turn):
             for index, (dy, shift) in enumerate(((1, 0), (3, 2), (2, 3), (0, 1))):
                 dz = (turn + shift) % SIDE
@@ -286,7 +288,7 @@
     def strip_part(k):
         return pl.ds(pl.multiple_of(rank * strip + PARTS[k][0] * height, height), height)
 
-    def to_owners(k):
+    def to_owners(k, turns):
         def visit(target):
             for slot in range(slots):
                 outgoing[k][target, slot] = reduced[k][block_of(target * slots + slot)]
@@ -298,7 +300,9 @@
                 device_id={"fsdp": target},
             ).start()
 
-        each_target(visit)
+        each_target(visit, turns)
+        if turns[0] > 0:
+            return
         for slot in range(slots):
             block[slot, strip_part(k), cols(k)] = reduced[k][block_of(rank * slots + slot)]
 
@@ -330,6 +334,8 @@
             near_sums(k + 1)
         if k + 2 < CHUNKS:
             far_sums(k + 2)
+        if k > 0:
+            to_owners(k - 1, (2, SIDE))
         if k + 1 < CHUNKS:
             relay(k + 1)
         if k == 1:
@@ -338,7 +344,8 @@
         if 1 <= k < CHUNKS - 2:
             moments(k - 1)
         finish(k)
-        to_owners(k)
+        to_owners(k, (0, 2))
+    to_owners(CHUNKS - 1, (2, SIDE))
     for k in range(CHUNKS - 3, CHUNKS):
         moments(k)
 
@@ -349,8 +356,6 @@
     for store in stores:
         store.start()
 
-    others = (ranks - 1) * strip
-
     def arrived(ref, sem):
         pltpu.make_async_copy(ref, ref, sem).wait()
 
@@ -359,57 +364,92 @@
     loads[0].wait()
     loads[1].wait()
 
-    for slot in range(slots):
-        product = jnp.dot(root_left[slot], block[slot], preferred_element_type=F32)
-        direction[slot] = jnp.dot(
-            product.astype(BF16), root_right[slot], preferred_element_type=F32
-        ).astype(BF16)
-
+    def first_legs(slot):
         for index, (first_leg, second_leg) in enumerate(legs_of(slot)):
             target = at_offset(first_leg[0] + second_leg[0], first_leg[1] + second_leg[1])
             pltpu.make_async_remote_copy(
                 src_ref=direction.at[slot, strip_rows(target)],
                 dst_ref=relayed.at[slot, index],
-                send_sem=back_send.at[slot],
+                send_sem=leg_send.at[slot],
                 recv_sem=relay_recv.at[slot, index],
                 device_id={"fsdp": at_offset(*first_leg)},
             ).start()
-        for offset in NEAR:
-            target = at_offset(*offset)
-            pltpu.make_async_remote_copy(
-                src_ref=direction.at[slot, strip_rows(target)],
-                dst_ref=returned.at[rank, slot],
-                send_sem=back_send.at[slot],
-                recv_sem=back_recv.at[slot],
-                device_id={"fsdp": target},
-            ).start()
-
-    for slot in range(slots):
+
+    def relays_arrived(slot):
+        for index in range(len(LEGS)):
+            arrived(relayed.at[slot, index], relay_recv.at[slot, index])
+
+    def second_legs(slot):
         for index, (first_leg, second_leg) in enumerate(legs_of(slot)):
             origin = at_offset(-first_leg[0], -first_leg[1])
-            arrived(relayed.at[slot, index], relay_recv.at[slot, index])
             pltpu.make_async_remote_copy(
                 src_ref=relayed.at[slot, index],
                 dst_ref=returned.at[origin, slot],
                 send_sem=relay_send.at[slot],
-                recv_sem=back_recv.at[slot],
+                recv_sem=last_recv.at[slot],
                 device_id={"fsdp": at_offset(*second_leg)},
             ).start()
 
-    for slot in range(slots):
-        keep = pltpu.make_async_copy(
-            direction.at[slot, strip_rows(rank)], returned.at[rank, slot], store_sem.at[4 + slot]
-        )
-        keep.start()
-        stores.append(keep)
+    def near_round(lo, hi):
+        for index in range(lo, hi):
+            target = at_offset(*NEAR[index])
+            pltpu.make_async_remote_copy(
+                src_ref=direction.at[:, strip_rows(target)],
+                dst_ref=returned.at[rank],
+                send_sem=back_send,
+                recv_sem=back_recv.at[index],
+                device_id={"fsdp": target},
+            ).start()
+
+    def near_arrived(lo, hi):
+        for index in range(lo, hi):
+            arrived(returned.at[rank], back_recv.at[index])
+
+    def precondition(slot):
+        product = jnp.dot(root_left[slot], block[slot], preferred_element_type=F32)
+        direction[slot] = jnp.dot(
+            product.astype(BF16), root_right[slot], preferred_element_type=F32
+        ).astype(BF16)
+
+    def sum_squares(slot):
         wide = direction[slot].astype(F32)
         wide = jnp.sum((wide * wide).reshape(-1, 8, columns), axis=0)
         sums[2 + slot] = functools.reduce(
             jnp.add, [wide[:, at : at + 128] for at in range(0, columns, 128)]
         )
+
+    def statistics(stat, contract, slot):
+        gram = lax.dot_general(
+            block[slot],
+            block[slot],
+            (((contract,), (contract,)), ((), ())),
+            preferred_element_type=F32,
+        )
+        used = held(rank * slots + slot) > 0
+        stat[slot] = 0.95 * stat[slot] + 0.05 * jnp.where(used, gram, 0.0)
+
+    precondition(0)
+    first_legs(0)
+    precondition(1)
+    first_legs(1)
+    sum_squares(0)
+    sum_squares(1)
     adam = jnp.sum(jnp.sum(adam_sums[...], axis=0), axis=1)
     for index in range(2):
         sums[index] = adam[index * 8 : index * 8 + 8]
+    relays_arrived(0)
+    near_round(0, 2)
+    near_round(2, 4)
+    loads[4].wait()
+    loads[5].wait()
+    relays_arrived(1)
+    near_round(4, 8)
+    statistics(stat_left, 1, 0)
+    near_arrived(0, 4)
+    second_legs(0)
+    statistics(stat_right, 0, 0)
+    near_arrived(4, 8)
+    second_legs(1)
 
     def send_sums(target):
         pltpu.make_async_remote_copy(
@@ -422,18 +462,15 @@
 
     each_target(send_sums)
     all_sums[rank] = sums[...]
-    loads[4].wait()
-    loads[5].wait()
-    for stat, contract, index, out in ((stat_left, 1, 2, left_out), (stat_right, 0, 3, right_out)):
-        for slot in range(slots):
-            gram = lax.dot_general(
-                block[slot],
-                block[slot],
-                (((contract,), (contract,)), ((), ())),
-                preferred_element_type=F32,
-            )
-            used = held(rank * slots + slot) > 0
-            stat[slot] = 0.95 * stat[slot] + 0.05 * jnp.where(used, gram, 0.0)
+    for slot in range(slots):
+        keep = pltpu.make_async_copy(
+            direction.at[slot, strip_rows(rank)], returned.at[rank, slot], store_sem.at[4 + slot]
+        )
+        keep.start()
+        stores.append(keep)
+    statistics(stat_left, 1, 1)
+    statistics(stat_right, 0, 1)
+    for stat, index, out in ((stat_left, 2, left_out), (stat_right, 3, right_out)):
         store = pltpu.make_async_copy(stat, out, store_sem.at[index])
         store.start()
         stores.append(store)
@@ -446,13 +483,12 @@
     adam_sq = jnp.sum(adam_sq, axis=1, keepdims=True)
     direction_sq = jnp.sum(jnp.sum(sizes[...], axis=1), axis=1, keepdims=True)
     graft[...] = jnp.broadcast_to(jnp.sqrt(adam_sq / (direction_sq + 1e-06)), graft.shape)
-
     for index, (src, out) in enumerate(((graft, graft_out), (places, places_out))):
         store = pltpu.make_async_copy(src, out, store_sem.at[6 + index])
         store.start()
         stores.append(store)
     for slot in range(slots):
-        arrived(returned.at[pl.ds(0, ranks - 1), slot], back_recv.at[slot])
+        arrived(relayed.at[slot], last_recv.at[slot])
 
     for k in chunks:
         for copy in ring_copies[k]:
@@ -461,8 +497,9 @@
         copy.wait_send()
     for k in chunks:
         arrived(outgoing[k].at[pl.ds(0, ranks - 1)], owner_send.at[k])
+    arrived(returned.at[pl.ds(0, len(NEAR))], back_send)
     for slot in range(slots):
-        arrived(direction.at[slot, pl.ds(0, others)], back_send.at[slot])
+        arrived(relayed.at[slot], leg_send.at[slot])
         arrived(relayed.at[slot], relay_send.at[slot])
     arrived(all_sums.at[pl.ds(0, ranks - 1)], sums_send)
     for store in stores:
@@ -529,10 +566,12 @@
             dma((CHUNKS, 6)),
             dma((CHUNKS,)),
             dma((CHUNKS,)),
-            dma((slots,)),
+            dma,
+            dma((len(NEAR),)),
             dma((slots,)),
             dma((slots,)),
             dma((slots, len(LEGS))),
+            dma((slots,)),
             dma,
             dma,
         ],

time: 58.4 us -> 61.2 us (1.048)
  Pallas kernels: 57.6 us -> 60.5 us
    pallas_call x1, Pallas kernels: 54.8 us -> 57.6 us  [exchange(): pl.pallas_call(exchange_kernel, out_shape=(jax.ShapeDtypeStruct((ranks, s...]
where the time goes in v5:
time: 61.2 us; the launch traced here: 61.1 us
  Pallas kernels  60.5 us (99%)
  between operations  0.64 us (1%)
    pallas_call x1, Pallas kernels, exchange(): pl.pallas_call(exchange_kernel, out_shape=(jax.ShapeDtypeStruct((ranks, s...  57.6 us
    pallas_call x1, Pallas kernels, publish(): pl.pallas_call(publish_kernel, out_shape=[jax.ShapeDtypeStruct(*shape) fo...  2.86 us

profile of v5, /device:TPU:0, one launch (start us, length us, event | category | flops | bytes accessed | tf_op | source)
XLA Modules:
  0.0 61.1 jit_solution(6974703644241913378)
XLA Ops:
  0.6 57.6 %exchange.1 = (bf16[16,2,32,512]{3,2,1,0:T(8,128)(2,1)S(1)}, f32[16,128]{1,0:T(8,128)S(1)}, s32[8,128]{1,0:T(8,128)S(1)}, f32[16,32,512]{2,1,0:T(8,128)S(1)}, f3...) custom-call(s32[1,128]{1,0:T(1,128)} %bitcast.3, ...), custom_call_target="tpu_custom_call" | custom-call | flops 2147483648 | bytes 18874368 | tf_op jit(solution)/shard_map/exchange/pallas_call | solution.py:519
  58.2 2.9 %publish.1 = (bf16[16,32,512]{2,1,0:T(8,128)(2,1)}, f32[16,32,512]{2,1,0:T(8,128)}, f32[16,32,512]{2,1,0:T(8,128)}, f32[2,512,512]{2,1,0:T(8,128)}, f32[2,512,512]{2,1,0:T(8,128)}) custom-call(bf16[16,2,32,512]{3,2,1,0:T(8,128)(2,1)S(1)} %get-tuple-element.12.returned, f32[16,128]{1,0:T(8,128)S(1)} %get-tuple-element.13.graft, ...), custom_call_target="tpu_custom_call" | custom-call | tf_op jit(solution)/shard_map/publish/pallas_call | solution.py:650

commit v6 on v4

--- a/solution.py
+++ b/solution.py
@@ -50,6 +50,7 @@
     places,
     place,
     own,
+    lend,
     other,
     pair,
     relay_right,
@@ -138,17 +139,16 @@
     owner_load = pltpu.make_async_copy(owner_ref, owner, place_sem.at[0])
     owner_load.start()
     order = (across, ahead, behind, x)
-    own_loads = {}
-    for part in range(2):
-        for index, line in enumerate(order):
-            there = pl.ds(part * height, height)
-            load = pltpu.make_async_copy(
-                grad_ref.at[line, core, :, there],
-                own.at[line, :, there],
-                own_sem.at[part, index],
-            )
-            load.start()
-            own_loads[part, index] = load
+    lend_loads, own_loads = [], []
+    for index, line in enumerate(order):
+        lend_loads.append(
+            pltpu.make_async_copy(grad_ref.at[line, 1 - core], lend.at[line], own_sem.at[0, index])
+        )
+        own_loads.append(
+            pltpu.make_async_copy(grad_ref.at[line, core], own.at[line], own_sem.at[1, index])
+        )
+    for load in lend_loads + own_loads:
+        load.start()
     loads = [
         pltpu.make_async_copy(src, dst, load_sem.at[index])
         for index, (src, dst) in enumerate(
@@ -193,19 +193,18 @@
 
     pl.semaphore_wait(barrier, ranks + 2)
 
-    core_copies = {}
-    for part in range(2):
-        for index, line in enumerate(order):
-            there = pl.ds(part * height, height)
-            copy = pltpu.make_async_remote_copy(
-                src_ref=grad_ref.at[line, 1 - core, :, there],
-                dst_ref=other.at[line, :, there],
-                send_sem=core_send.at[part, index],
-                recv_sem=core_recv.at[part, line],
-                device_id={"dp": mate},
-            )
-            copy.start()
-            core_copies[part, index] = copy
+    core_copies = []
+    for index, line in enumerate(order):
+        lend_loads[index].wait()
+        copy = pltpu.make_async_remote_copy(
+            src_ref=lend.at[line],
+            dst_ref=other.at[line],
+            send_sem=core_send.at[index],
+            recv_sem=core_recv.at[line],
+            device_id={"dp": mate},
+        )
+        copy.start()
+        core_copies.append(copy)
     place_copy.wait()
 
     def held(at):
@@ -218,11 +217,10 @@
         return jnp.clip(place[0, dp * per_group + index], 0, ranks * slots - 1)
 
     def ready(k, index):
-        if PARTS[k][1] == 0:
-            part, line = PARTS[k][0], order[index]
-            own_loads[part, index].wait()
-            ref = other.at[line, :, upper(k)]
-            pltpu.make_async_copy(ref, ref, core_recv.at[part, line]).wait()
+        if k == 0:
+            line = order[index]
+            own_loads[index].wait()
+            pltpu.make_async_copy(other.at[line], other.at[line], core_recv.at[line]).wait()
 
     def both(k, index):
         line = order[index]
@@ -457,7 +455,7 @@
     for k in chunks:
         for copy in ring_copies[k]:
             copy.wait_send()
-    for copy in core_copies.values():
+    for copy in core_copies:
         copy.wait_send()
     for k in chunks:
         arrived(outgoing[k].at[pl.ds(0, ranks - 1)], owner_send.at[k])
@@ -498,6 +496,7 @@
             pltpu.SMEM((8, 128), I32),
             vmem((lines, per_group, strip, columns), BF16),
             vmem((lines, per_group, strip, columns), BF16),
+            vmem((lines, per_group, strip, columns), BF16),
             [vmem((lines, per_group, height, wide), BF16) for wide in widths],
             [vmem((half, height, wide), BF16) for wide in widths],
             [vmem((half, height, wide), BF16) for wide in widths],
@@ -523,8 +522,8 @@
             dma((2, 4)),
             dma((6,)),
             dma((8,)),
-            dma((2, 4)),
-            dma((2, 4)),
+            dma((4,)),
+            dma((4,)),
             dma((CHUNKS, 6)),
             dma((CHUNKS, 6)),
             dma((CHUNKS,)),

time: 58.4 us -> 58.5 us (level)
  no operation moved by 1% of the time
where the time goes in v6:
time: 58.5 us; the launch traced here: 58.3 us
  Pallas kernels  57.7 us (99%)
  between operations  0.64 us (1%)
    pallas_call x1, Pallas kernels, exchange(): pl.pallas_call(exchange_kernel, out_shape=(jax.ShapeDtypeStruct((ranks, s...  54.8 us
    pallas_call x1, Pallas kernels, publish(): pl.pallas_call(publish_kernel, out_shape=[jax.ShapeDtypeStruct(*shape) fo...  2.86 us

profile of v6, /device:TPU:0, one launch (start us, length us, event | category | flops | bytes accessed | tf_op | source)
XLA Modules:
  0.0 58.3 jit_solution(16567132875485829867)
XLA Ops:
  0.6 54.8 %exchange.1 = (bf16[16,2,32,512]{3,2,1,0:T(8,128)(2,1)S(1)}, f32[16,128]{1,0:T(8,128)S(1)}, s32[8,128]{1,0:T(8,128)S(1)}, f32[16,32,512]{2,1,0:T(8,128)S(1)}, f3...) custom-call(s32[1,128]{1,0:T(1,128)} %bitcast.3, ...), custom_call_target="tpu_custom_call" | custom-call | flops 2147483648 | bytes 18874368 | tf_op jit(solution)/shard_map/exchange/pallas_call | solution.py:480
  55.5 2.9 %publish.1 = (bf16[16,32,512]{2,1,0:T(8,128)(2,1)}, f32[16,32,512]{2,1,0:T(8,128)}, f32[16,32,512]{2,1,0:T(8,128)}, f32[2,512,512]{2,1,0:T(8,128)}, f32[2,512,512]{2,1,0:T(8,128)}) custom-call(bf16[16,2,32,512]{3,2,1,0:T(8,128)(2,1)S(1)} %get-tuple-element.12.returned, f32[16,128]{1,0:T(8,128)S(1)} %get-tuple-element.13.graft, ...), custom_call_target="tpu_custom_call" | custom-call | tf_op jit(solution)/shard_map/publish/pallas_call | solution.py:610

commit v7 on v6

--- a/solution.py
+++ b/solution.py
@@ -40,14 +40,13 @@
     left_ref,
     right_ref,
     returned,
-    graft_out,
-    places_out,
+    graft,
+    places,
     first_out,
     second_out,
     left_out,
     right_out,
     owner,
-    places,
     place,
     own,
     lend,
@@ -71,12 +70,10 @@
     sums,
     all_sums,
     sizes,
-    graft,
     adam_sums,
     place_sem,
     own_sem,
     load_sem,
-    store_sem,
     core_send,
     core_recv,
     ring_send,
@@ -186,8 +183,9 @@
     held_row = jnp.sum(
         jnp.where(along.astype(F32) == place_col, number, 0.0), axis=0, keepdims=True
     )
-    places[0:1] = place_row.astype(I32)
-    places[1:2] = held_row.astype(I32)
+    places[...] = jnp.concatenate(
+        [place_row, held_row, jnp.zeros((6, count), F32)], axis=0
+    ).astype(I32)
     place_copy = pltpu.make_async_copy(places, place, place_sem.at[1])
     place_copy.start()
 
@@ -309,8 +307,8 @@
             grad = reduced[k][here].astype(F32)
             first_new = 0.9 * first[here, upper(k), cols(k)] + 0.1 * grad
             second_new = 0.95 * second[here, upper(k), cols(k)] + 0.05 * grad * grad
-            first[here, upper(k), cols(k)] = first_new
-            second[here, upper(k), cols(k)] = second_new
+            first_out[here, upper(k), cols(k)] = first_new
+            second_out[here, upper(k), cols(k)] = second_new
             adam = first_new / (jnp.sqrt(second_new) + 1e-08)
             adam = jnp.sum((adam * adam).reshape(step, height // 8, 8, -1), axis=1)
             adam_sums[k, here] = functools.reduce(
@@ -340,15 +338,6 @@
     for k in range(CHUNKS - 3, CHUNKS):
         moments(k)
 
-    stores = [
-        pltpu.make_async_copy(first, first_out, store_sem.at[0]),
-        pltpu.make_async_copy(second, second_out, store_sem.at[1]),
-    ]
-    for store in stores:
-        store.start()
-
-    others = (ranks - 1) * strip
-
     def arrived(ref, sem):
         pltpu.make_async_copy(ref, ref, sem).wait()
 
@@ -395,11 +384,7 @@
             ).start()
 
     for slot in range(slots):
-        keep = pltpu.make_async_copy(
-            direction.at[slot, strip_rows(rank)], returned.at[rank, slot], store_sem.at[4 + slot]
-        )
-        keep.start()
-        stores.append(keep)
+        returned[rank, slot] = direction[slot, strip_rows(rank)]
         wide = direction[slot].astype(F32)
         wide = jnp.sum((wide * wide).reshape(-1, 8, columns), axis=0)
         sums[2 + slot] = functools.reduce(
@@ -422,7 +407,7 @@
     all_sums[rank] = sums[...]
     loads[4].wait()
     loads[5].wait()
-    for stat, contract, index, out in ((stat_left, 1, 2, left_out), (stat_right, 0, 3, right_out)):
+    for stat, contract, out in ((stat_left, 1, left_out), (stat_right, 0, right_out)):
         for slot in range(slots):
             gram = lax.dot_general(
                 block[slot],
@@ -431,10 +416,7 @@
                 preferred_element_type=F32,
             )
             used = held(rank * slots + slot) > 0
-            stat[slot] = 0.95 * stat[slot] + 0.05 * jnp.where(used, gram, 0.0)
-        store = pltpu.make_async_copy(stat, out, store_sem.at[index])
-        store.start()
-        stores.append(store)
+            out[slot] = 0.95 * stat[slot] + 0.05 * jnp.where(used, gram, 0.0)
 
     arrived(all_sums.at[pl.ds(0, ranks - 1)], sums_recv)
     for index in range(per_group):
@@ -445,10 +427,6 @@
     direction_sq = jnp.sum(jnp.sum(sizes[...], axis=1), axis=1, keepdims=True)
     graft[...] = jnp.broadcast_to(jnp.sqrt(adam_sq / (direction_sq + 1e-06)), graft.shape)
 
-    for index, (src, out) in enumerate(((graft, graft_out), (places, places_out))):
-        store = pltpu.make_async_copy(src, out, store_sem.at[6 + index])
-        store.start()
-        stores.append(store)
     for slot in range(slots):
         arrived(returned.at[pl.ds(0, ranks - 1), slot], back_recv.at[slot])
 
@@ -460,11 +438,9 @@
     for k in chunks:
         arrived(outgoing[k].at[pl.ds(0, ranks - 1)], owner_send.at[k])
     for slot in range(slots):
-        arrived(direction.at[slot, pl.ds(0, others)], back_send.at[slot])
+        arrived(direction.at[slot, pl.ds(0, (ranks - 1) * strip)], back_send.at[slot])
         arrived(relayed.at[slot], relay_send.at[slot])
     arrived(all_sums.at[pl.ds(0, ranks - 1)], sums_send)
-    for store in stores:
-        store.wait()
 
 
 def exchange(block_owner, gradients, root_left, root_right, first, second, left, right, ranks):
@@ -473,26 +449,24 @@
     height = strip // 2
     widths = [tiles * 128 for _, _, tiles in PARTS]
     half = per_group // 2
-    anywhere = pl.BlockSpec(memory_space=pl.ANY)
     far = pl.BlockSpec(memory_space=pltpu.HBM)
     dma = pltpu.SemaphoreType.DMA
     vmem = pltpu.VMEM
     return pl.pallas_call(
         exchange_kernel,
         out_shape=(
-            jax.ShapeDtypeStruct((ranks, slots, strip, columns), BF16),
-            jax.ShapeDtypeStruct((per_group, 128), F32),
-            jax.ShapeDtypeStruct((8, 128), I32),
-            jax.ShapeDtypeStruct(first.shape, F32),
-            jax.ShapeDtypeStruct(first.shape, F32),
-            jax.ShapeDtypeStruct(left.shape, F32),
-            jax.ShapeDtypeStruct(right.shape, F32),
+            pltpu.VMEM((ranks, slots, strip, columns), BF16),
+            pltpu.VMEM((per_group, 128), F32),
+            pltpu.VMEM((8, 128), I32),
+            pltpu.VMEM(first.shape, F32),
+            pltpu.VMEM(first.shape, F32),
+            pltpu.VMEM(left.shape, F32),
+            pltpu.VMEM(right.shape, F32),
         ),
         in_specs=[far] * 8,
-        out_specs=(anywhere,) * 7,
+        out_specs=(pl.BlockSpec(memory_space=pltpu.VMEM),) * 7,
         scratch_shapes=[
             vmem(block_owner.shape, I32),
-            vmem((8, 128), I32),
             pltpu.SMEM((8, 128), I32),
             vmem((lines, per_group, strip, columns), BF16),
             vmem((lines, per_group, strip, columns), BF16),
@@ -516,12 +490,10 @@
             vmem((4, 8, 128), F32),
             vmem((ranks, 4, 8, 128), F32),
             vmem((per_group, 8, 128), F32),
-            vmem((per_group, 128), F32),
             vmem((CHUNKS, per_group, 8, 128), F32),
             dma((2,)),
             dma((2, 4)),
             dma((6,)),
-            dma((8,)),
             dma((4,)),
             dma((4,)),
             dma((CHUNKS, 6)),

time: 58.5 us -> 58.3 us (level)
  no operation moved by 1% of the time
where the time goes in v7:
time: 58.3 us; the launch traced here: 58.2 us
  Pallas kernels  57.5 us (99%)
  between operations  0.64 us (1%)
    pallas_call x1, Pallas kernels, exchange(): pl.pallas_call(exchange_kernel, out_shape=(pltpu.VMEM((ranks, slots, stri...  54.7 us
    pallas_call x1, Pallas kernels, publish(): pl.pallas_call(publish_kernel, out_shape=[jax.ShapeDtypeStruct(*shape) fo...  2.86 us

profile of v7, /device:TPU:0, one launch (start us, length us, event | category | flops | bytes accessed | tf_op | source)
XLA Modules:
  0.0 58.2 jit_solution(6900009597232267633)
XLA Ops:
  0.6 54.7 %exchange.1 = (bf16[16,2,32,512]{3,2,1,0:T(8,128)(2,1)S(1)}, f32[16,128]{1,0:T(8,128)S(1)}, s32[8,128]{1,0:T(8,128)S(1)}, f32[16,32,512]{2,1,0:T(8,128)S(1)}, f3...) custom-call(s32[1,128]{1,0:T(1,128)} %bitcast.3, ...), custom_call_target="tpu_custom_call" | custom-call | flops 2147483648 | bytes 18874368 | tf_op jit(solution)/shard_map/exchange/pallas_call | solution.py:455
  55.3 2.9 %publish.1 = (bf16[16,32,512]{2,1,0:T(8,128)(2,1)}, f32[16,32,512]{2,1,0:T(8,128)}, f32[16,32,512]{2,1,0:T(8,128)}, f32[2,512,512]{2,1,0:T(8,128)}, f32[2,512,512]{2,1,0:T(8,128)}) custom-call(bf16[16,2,32,512]{3,2,1,0:T(8,128)(2,1)S(1)} %get-tuple-element.12.returned, f32[16,128]{1,0:T(8,128)S(1)} %get-tuple-element.13.graft, ...), custom_call_target="tpu_custom_call" | custom-call | tf_op jit(solution)/shard_map/publish/pallas_call | solution.py:582

commit v8 on v7

--- a/solution.py
+++ b/solution.py
@@ -346,12 +346,13 @@
     loads[0].wait()
     loads[1].wait()
 
-    for slot in range(slots):
+    def precondition(slot):
         product = jnp.dot(root_left[slot], block[slot], preferred_element_type=F32)
         direction[slot] = jnp.dot(
             product.astype(BF16), root_right[slot], preferred_element_type=F32
         ).astype(BF16)
 
+    def first_legs(slot):
         for index, (first_leg, second_leg) in enumerate(legs_of(slot)):
             target = at_offset(first_leg[0] + second_leg[0], first_leg[1] + second_leg[1])
             pltpu.make_async_remote_copy(
@@ -361,6 +362,8 @@
                 recv_sem=relay_recv.at[slot, index],
                 device_id={"fsdp": at_offset(*first_leg)},
             ).start()
+
+    def direct(slot):
         for offset in NEAR:
             target = at_offset(*offset)
             pltpu.make_async_remote_copy(
@@ -370,8 +373,9 @@
                 recv_sem=back_recv.at[slot],
                 device_id={"fsdp": target},
             ).start()
-
-    for slot in range(slots):
+        returned[rank, slot] = direction[slot, strip_rows(rank)]
+
+    def second_legs(slot):
         for index, (first_leg, second_leg) in enumerate(legs_of(slot)):
             origin = at_offset(-first_leg[0], -first_leg[1])
             arrived(relayed.at[slot, index], relay_recv.at[slot, index])
@@ -383,16 +387,10 @@
                 device_id={"fsdp": at_offset(*second_leg)},
             ).start()
 
-    for slot in range(slots):
-        returned[rank, slot] = direction[slot, strip_rows(rank)]
+    def squares(slot):
         wide = direction[slot].astype(F32)
-        wide = jnp.sum((wide * wide).reshape(-1, 8, columns), axis=0)
-        sums[2 + slot] = functools.reduce(
-            jnp.add, [wide[:, at : at + 128] for at in range(0, columns, 128)]
-        )
-    adam = jnp.sum(jnp.sum(adam_sums[...], axis=0), axis=1)
-    for index in range(2):
-        sums[index] = adam[index * 8 : index * 8 + 8]
+        wide = jnp.sum(jnp.sum((wide * wide).reshape(-1, 8, columns), axis=0), axis=0, keepdims=True)
+        return jnp.sum(wide, axis=1, keepdims=True)
 
     def send_sums(target):
         pltpu.make_async_remote_copy(
@@ -403,8 +401,23 @@
             device_id={"fsdp": target},
         ).start()
 
+    adam = jnp.sum(jnp.sum(jnp.sum(adam_sums[...], axis=0), axis=1), axis=1, keepdims=True)
+    lane = lax.broadcasted_iota(I32, (8, 128), 1)
+    precondition(0)
+    first_legs(0)
+    direct(0)
+    precondition(1)
+    first_legs(1)
+    tile = jnp.where(lane == 0, adam[:8], 0.0) + jnp.where(lane == 1, adam[8:], 0.0)
+    for slot in range(slots):
+        tile = tile + jnp.where(lane == 2 + slot, squares(slot), 0.0)
+    sums[...] = tile
+    all_sums[rank] = tile
     each_target(send_sums)
-    all_sums[rank] = sums[...]
+    direct(1)
+    second_legs(0)
+    second_legs(1)
+
     loads[4].wait()
     loads[5].wait()
     for stat, contract, out in ((stat_left, 1, left_out), (stat_right, 0, right_out)):
@@ -421,12 +434,12 @@
     arrived(all_sums.at[pl.ds(0, ranks - 1)], sums_recv)
     for index in range(per_group):
         at = place_of(index)
-        sizes[index] = all_sums[at // slots, 2 + at % slots]
-    adam_sq = jnp.sum(all_sums[:, 0:2], axis=0).reshape(per_group, 128)
-    adam_sq = jnp.sum(adam_sq, axis=1, keepdims=True)
-    direction_sq = jnp.sum(jnp.sum(sizes[...], axis=1), axis=1, keepdims=True)
+        row = all_sums[at // slots, pl.ds(0, 1)]
+        sizes[index : index + 1] = jnp.where(lane[:1] == 2 + at % slots, row, 0.0)
+    total = jnp.sum(all_sums[...], axis=0)
+    adam_sq = jnp.concatenate([total[:, 0:1], total[:, 1:2]], axis=0)
+    direction_sq = jnp.sum(sizes[...], axis=1, keepdims=True)
     graft[...] = jnp.broadcast_to(jnp.sqrt(adam_sq / (direction_sq + 1e-06)), graft.shape)
-
     for slot in range(slots):
         arrived(returned.at[pl.ds(0, ranks - 1), slot], back_recv.at[slot])
 
@@ -487,9 +500,9 @@
             vmem(right.shape, F32),
             vmem((slots, rows, columns), BF16),
             vmem((slots, len(LEGS), strip, columns), BF16),
-            vmem((4, 8, 128), F32),
-            vmem((ranks, 4, 8, 128), F32),
-            vmem((per_group, 8, 128), F32),
+            vmem((8, 128), F32),
+            vmem((ranks, 8, 128), F32),
+            vmem((per_group, 128), F32),
             vmem((CHUNKS, per_group, 8, 128), F32),
             dma((2,)),
             dma((2, 4)),

time: 58.3 us -> 55.8 us (0.957)
  Pallas kernels: 57.5 us -> 55 us
    pallas_call x1, Pallas kernels: 54.7 us -> 52.2 us  [exchange(): pl.pallas_call(exchange_kernel, out_shape=(pltpu.VMEM((ranks, slots, stri...]
where the time goes in v8:
time: 55.8 us; the launch traced here: 55.7 us
  Pallas kernels  55 us (99%)
  between operations  0.64 us (1%)
    pallas_call x1, Pallas kernels, exchange(): pl.pallas_call(exchange_kernel, out_shape=(pltpu.VMEM((ranks, slots, stri...  52.2 us
    pallas_call x1, Pallas kernels, publish(): pl.pallas_call(publish_kernel, out_shape=[jax.ShapeDtypeStruct(*shape) fo...  2.86 us

profile of v8, /device:TPU:0, one launch (start us, length us, event | category | flops | bytes accessed | tf_op | source)
XLA Modules:
  0.0 55.7 jit_solution(1527638288526902797)
XLA Ops:
  0.6 52.2 %exchange.1 = (bf16[16,2,32,512]{3,2,1,0:T(8,128)(2,1)S(1)}, f32[16,128]{1,0:T(8,128)S(1)}, s32[8,128]{1,0:T(8,128)S(1)}, f32[16,32,512]{2,1,0:T(8,128)S(1)}, f3...) custom-call(s32[1,128]{1,0:T(1,128)} %bitcast.3, ...), custom_call_target="tpu_custom_call" | custom-call | flops 2147483648 | bytes 18874368 | tf_op jit(solution)/shard_map/exchange/pallas_call | solution.py:468
  52.8 2.9 %publish.1 = (bf16[16,32,512]{2,1,0:T(8,128)(2,1)}, f32[16,32,512]{2,1,0:T(8,128)}, f32[16,32,512]{2,1,0:T(8,128)}, f32[2,512,512]{2,1,0:T(8,128)}, f32[2,512,512]{2,1,0:T(8,128)}) custom-call(bf16[16,2,32,512]{3,2,1,0:T(8,128)(2,1)S(1)} %get-tuple-element.12.returned, f32[16,128]{1,0:T(8,128)S(1)} %get-tuple-element.13.graft, ...), custom_call_target="tpu_custom_call" | custom-call | tf_op jit(solution)/shard_map/publish/pallas_call | solution.py:595

commit v9 on v8

--- a/solution.py
+++ b/solution.py
@@ -13,21 +13,10 @@
 PARTS = ((0, 0, 1), (0, 1, 1), (0, 2, 2), (1, 0, 2), (1, 2, 1), (1, 3, 1))
 CHUNKS = len(PARTS)
 SIDE = 4
-NEAR = ((1, 0), (-1, 0), (0, 1), (0, -1), (1, 1), (-1, -1), (1, -1), (-1, 1))
-LEGS = (
-    ((1, 1), (1, 1)),
-    ((-1, 1), (-1, 0)),
-    ((-1, -1), (-1, 0)),
-    ((1, -1), (0, -1)),
-    ((-1, -1), (0, -1)),
-    ((1, 0), (1, 0)),
-    ((0, 1), (0, 1)),
+OFFSETS = (
+    *((2, 2), (2, 1), (2, -1), (1, 2), (-1, 2), (2, 0), (0, 2)),
+    *((1, 1), (-1, -1), (1, -1), (-1, 1), (1, 0), (-1, 0), (0, 1), (0, -1)),
 )
-
-
-def legs_of(slot):
-    sign = 1 - 2 * slot
-    return [tuple((sign * dy, sign * dz) for dy, dz in legs) for legs in LEGS]
 
 
 def exchange_kernel(
@@ -66,7 +55,6 @@
     stat_left,
     stat_right,
     direction,
-    relayed,
     sums,
     all_sums,
     sizes,
@@ -82,8 +70,6 @@
     owner_recv,
     back_send,
     back_recv,
-    relay_send,
-    relay_recv,
     sums_send,
     sums_recv,
 ):
@@ -192,13 +178,16 @@
     pl.semaphore_wait(barrier, ranks + 2)
 
     core_copies = []
-    for index, line in enumerate(order):
-        lend_loads[index].wait()
+    everything, top, bottom = pl.ds(0, strip), pl.ds(0, height), pl.ds(height, height)
+    pieces = ((0, top), (0, bottom), (1, everything), (2, everything), (3, everything))
+    for at, (index, there) in enumerate(pieces):
+        if at != 1:
+            lend_loads[index].wait()
         copy = pltpu.make_async_remote_copy(
-            src_ref=lend.at[line],
-            dst_ref=other.at[line],
-            send_sem=core_send.at[index],
-            recv_sem=core_recv.at[line],
+            src_ref=lend.at[order[index], :, there],
+            dst_ref=other.at[order[index], :, there],
+            send_sem=core_send.at[at],
+            recv_sem=core_recv.at[lines if at == 1 else order[index]],
             device_id={"dp": mate},
         )
         copy.start()
@@ -216,9 +205,12 @@
 
     def ready(k, index):
         if k == 0:
-            line = order[index]
             own_loads[index].wait()
-            pltpu.make_async_copy(other.at[line], other.at[line], core_recv.at[line]).wait()
+        if PARTS[k][1] == 0 and (k == 0 or index == 0):
+            at = index + 1 if index else PARTS[k][0]
+            ref = other.at[order[index], :, pieces[at][1]]
+            sem = core_recv.at[lines if at == 1 else order[index]]
+            pltpu.make_async_copy(ref, ref, sem).wait()
 
     def both(k, index):
         line = order[index]
@@ -352,19 +344,8 @@
             product.astype(BF16), root_right[slot], preferred_element_type=F32
         ).astype(BF16)
 
-    def first_legs(slot):
-        for index, (first_leg, second_leg) in enumerate(legs_of(slot)):
-            target = at_offset(first_leg[0] + second_leg[0], first_leg[1] + second_leg[1])
-            pltpu.make_async_remote_copy(
-                src_ref=direction.at[slot, strip_rows(target)],
-                dst_ref=relayed.at[slot, index],
-                send_sem=back_send.at[slot],
-                recv_sem=relay_recv.at[slot, index],
-                device_id={"fsdp": at_offset(*first_leg)},
-            ).start()
-
-    def direct(slot):
-        for offset in NEAR:
+    def send_back(slot):
+        for offset in OFFSETS:
             target = at_offset(*offset)
             pltpu.make_async_remote_copy(
                 src_ref=direction.at[slot, strip_rows(target)],
@@ -375,18 +356,6 @@
             ).start()
         returned[rank, slot] = direction[slot, strip_rows(rank)]
 
-    def second_legs(slot):
-        for index, (first_leg, second_leg) in enumerate(legs_of(slot)):
-            origin = at_offset(-first_leg[0], -first_leg[1])
-            arrived(relayed.at[slot, index], relay_recv.at[slot, index])
-            pltpu.make_async_remote_copy(
-                src_ref=relayed.at[slot, index],
-                dst_ref=returned.at[origin, slot],
-                send_sem=relay_send.at[slot],
-                recv_sem=back_recv.at[slot],
-                device_id={"fsdp": at_offset(*second_leg)},
-            ).start()
-
     def squares(slot):
         wide = direction[slot].astype(F32)
         wide = jnp.sum(jnp.sum((wide * wide).reshape(-1, 8, columns), axis=0), axis=0, keepdims=True)
@@ -404,19 +373,15 @@
     adam = jnp.sum(jnp.sum(jnp.sum(adam_sums[...], axis=0), axis=1), axis=1, keepdims=True)
     lane = lax.broadcasted_iota(I32, (8, 128), 1)
     precondition(0)
-    first_legs(0)
-    direct(0)
+    send_back(0)
     precondition(1)
-    first_legs(1)
     tile = jnp.where(lane == 0, adam[:8], 0.0) + jnp.where(lane == 1, adam[8:], 0.0)
     for slot in range(slots):
         tile = tile + jnp.where(lane == 2 + slot, squares(slot), 0.0)
     sums[...] = tile
     all_sums[rank] = tile
     each_target(send_sums)
-    direct(1)
-    second_legs(0)
-    second_legs(1)
+    send_back(1)
 
     loads[4].wait()
     loads[5].wait()
@@ -452,7 +417,6 @@
         arrived(outgoing[k].at[pl.ds(0, ranks - 1)], owner_send.at[k])
     for slot in range(slots):
         arrived(direction.at[slot, pl.ds(0, (ranks - 1) * strip)], back_send.at[slot])
-        arrived(relayed.at[slot], relay_send.at[slot])
     arrived(all_sums.at[pl.ds(0, ranks - 1)], sums_send)
 
 
@@ -499,7 +463,6 @@
             vmem(left.shape, F32),
             vmem(right.shape, F32),
             vmem((slots, rows, columns), BF16),
-            vmem((slots, len(LEGS), strip, columns), BF16),
             vmem((8, 128), F32),
             vmem((ranks, 8, 128), F32),
             vmem((per_group, 128), F32),
@@ -507,16 +470,14 @@
             dma((2,)),
             dma((2, 4)),
             dma((6,)),
-            dma((4,)),
-            dma((4,)),
+            dma((5,)),
+            dma((5,)),
             dma((CHUNKS, 6)),
             dma((CHUNKS, 6)),
             dma((CHUNKS,)),
             dma((CHUNKS,)),
             dma((slots,)),
             dma((slots,)),
-            dma((slots,)),
-            dma((slots, len(LEGS))),
             dma,
             dma,
         ],

time: 55.8 us -> 55.5 us (level)
  no operation moved by 1% of the time
where the time goes in v9:
time: 55.5 us; the launch traced here: 55.4 us
  Pallas kernels  54.7 us (99%)
  between operations  0.64 us (1%)
    pallas_call x1, Pallas kernels, exchange(): pl.pallas_call(exchange_kernel, out_shape=(pltpu.VMEM((ranks, slots, stri...  51.9 us
    pallas_call x1, Pallas kernels, publish(): pl.pallas_call(publish_kernel, out_shape=[jax.ShapeDtypeStruct(*shape) fo...  2.86 us

profile of v9, /device:TPU:0, one launch (start us, length us, event | category | flops | bytes accessed | tf_op | source)
XLA Modules:
  0.0 55.4 jit_solution(18312548074015470121)
XLA Ops:
  0.6 51.9 %exchange.1 = (bf16[16,2,32,512]{3,2,1,0:T(8,128)(2,1)S(1)}, f32[16,128]{1,0:T(8,128)S(1)}, s32[8,128]{1,0:T(8,128)S(1)}, f32[16,32,512]{2,1,0:T(8,128)S(1)}, f3...) custom-call(s32[1,128]{1,0:T(1,128)} %bitcast.3, ...), custom_call_target="tpu_custom_call" | custom-call | flops 2147483648 | bytes 18874368 | tf_op jit(solution)/shard_map/exchange/pallas_call | solution.py:432
  52.5 2.9 %publish.1 = (bf16[16,32,512]{2,1,0:T(8,128)(2,1)}, f32[16,32,512]{2,1,0:T(8,128)}, f32[16,32,512]{2,1,0:T(8,128)}, f32[2,512,512]{2,1,0:T(8,128)}, f32[2,512,512]{2,1,0:T(8,128)}) custom-call(bf16[16,2,32,512]{3,2,1,0:T(8,128)(2,1)S(1)} %get-tuple-element.12.returned, f32[16,128]{1,0:T(8,128)S(1)} %get-tuple-element.13.graft, ...), custom_call_target="tpu_custom_call" | custom-call | tf_op jit(solution)/shard_map/publish/pallas_call | solution.py:556

commit v10 on v9

--- a/solution.py
+++ b/solution.py
@@ -10,8 +10,9 @@
 F32 = jnp.float32
 BF16 = jnp.bfloat16
 I32 = jnp.int32
-PARTS = ((0, 0, 1), (0, 1, 1), (0, 2, 2), (1, 0, 2), (1, 2, 1), (1, 3, 1))
+PARTS = ((0, 0, 1), (0, 1, 1), (1, 0, 2), (0, 2, 2), (1, 2, 1), (1, 3, 1))
 CHUNKS = len(PARTS)
+EARLY = 3
 SIDE = 4
 OFFSETS = (
     *((2, 2), (2, 1), (2, -1), (1, 2), (-1, 2), (2, 0), (0, 2)),
@@ -54,6 +55,7 @@
     second,
     stat_left,
     stat_right,
+    partial,
     direction,
     sums,
     all_sums,
@@ -327,22 +329,30 @@
             moments(k - 1)
         finish(k)
         to_owners(k)
+    def arrived(ref, sem):
+        pltpu.make_async_copy(ref, ref, sem).wait()
+
+    def owners_have(k):
+        arrived(outgoing[k].at[pl.ds(0, ranks - 1)], owner_recv.at[k])
+
+    def part_product(slot, there):
+        part = jnp.dot(root_left[slot], block[slot, :, there], preferred_element_type=F32)
+        return jnp.dot(part.astype(BF16), root_right[slot, there], preferred_element_type=F32)
+
+    front, back = pl.ds(0, columns // 2), pl.ds(columns // 2, columns // 2)
+    loads[0].wait()
+    loads[1].wait()
+    for k in range(EARLY):
+        owners_have(k)
+    for slot in range(slots):
+        partial[slot] = part_product(slot, front)
     for k in range(CHUNKS - 3, CHUNKS):
         moments(k)
-
-    def arrived(ref, sem):
-        pltpu.make_async_copy(ref, ref, sem).wait()
-
-    for k in chunks:
-        arrived(outgoing[k].at[pl.ds(0, ranks - 1)], owner_recv.at[k])
-    loads[0].wait()
-    loads[1].wait()
+    for k in range(EARLY, CHUNKS):
+        owners_have(k)
 
     def precondition(slot):
-        product = jnp.dot(root_left[slot], block[slot], preferred_element_type=F32)
-        direction[slot] = jnp.dot(
-            product.astype(BF16), root_right[slot], preferred_element_type=F32
-        ).astype(BF16)
+        direction[slot] = (partial[slot] + part_product(slot, back)).astype(BF16)
 
     def send_back(slot):
         for offset in OFFSETS:
@@ -462,6 +472,7 @@
             vmem(first.shape, F32),
             vmem(left.shape, F32),
             vmem(right.shape, F32),
+            vmem((slots, rows, columns), F32),
             vmem((slots, rows, columns), BF16),
             vmem((8, 128), F32),
             vmem((ranks, 8, 128), F32),
@@ -524,12 +535,17 @@
 ):
     per_group, strip, columns = update.shape
     ranks, slots = returned.shape[:2]
-    place_copy = pltpu.make_async_copy(places, place, sems.at[5])
+    place_copy = pltpu.make_async_copy(places, place, sems.at[9])
     place_copy.start()
     pairs = ((left, left_out), (right, right_out), (first, first_out), (second, second_out))
-    copies = [
-        pltpu.make_async_copy(src, out, sems.at[index]) for index, (src, out) in enumerate(pairs)
-    ]
+    copies = []
+    for index, (src, out) in enumerate(pairs):
+        part = src.shape[0] // 2
+        for at in range(2):
+            here = pl.ds(at * part, part)
+            copies.append(
+                pltpu.make_async_copy(src.at[here], out.at[here], sems.at[2 * index + at])
+            )
     for copy in copies:
         copy.start()
     place_copy.wait()
@@ -542,7 +558,7 @@
         value = returned[at // slots, at % slots].astype(F32)
         update[index] = (value * jnp.concatenate([scale] * (columns // 128), axis=1)).astype(BF16)
 
-    copies.append(pltpu.make_async_copy(update, update_out, sems.at[4]))
+    copies.append(pltpu.make_async_copy(update, update_out, sems.at[8]))
     copies[-1].start()
     for copy in copies:
         copy.wait()
@@ -561,7 +577,7 @@
         scratch_shapes=[
             pltpu.SMEM((8, 128), I32),
             pltpu.VMEM(first.shape, BF16),
-            pltpu.SemaphoreType.DMA((6,)),
+            pltpu.SemaphoreType.DMA((10,)),
         ],
         compiler_params=pltpu.CompilerParams(vmem_limit_bytes=4 * 2**20),
         name="publish",

time: 55.5 us -> 55.5 us (level)
  no operation moved by 1% of the time
where the time goes in v10:
time: 55.5 us; the launch traced here: 55.4 us
  Pallas kernels  54.7 us (99%)
  between operations  0.64 us (1%)
    pallas_call x1, Pallas kernels, exchange(): pl.pallas_call(exchange_kernel, out_shape=(pltpu.VMEM((ranks, slots, stri...  51.8 us
    pallas_call x1, Pallas kernels, publish(): pl.pallas_call(publish_kernel, out_shape=[jax.ShapeDtypeStruct(*shape) fo...  2.89 us

profile of v10, /device:TPU:0, one launch (start us, length us, event | category | flops | bytes accessed | tf_op | source)
XLA Modules:
  0.0 55.4 jit_solution(13542377496253084840)
XLA Ops:
  0.6 51.8 %exchange.1 = (bf16[16,2,32,512]{3,2,1,0:T(8,128)(2,1)S(1)}, f32[16,128]{1,0:T(8,128)S(1)}, s32[8,128]{1,0:T(8,128)S(1)}, f32[16,32,512]{2,1,0:T(8,128)S(1)}, f3...) custom-call(s32[1,128]{1,0:T(1,128)} %bitcast.3, ...), custom_call_target="tpu_custom_call" | custom-call | flops 2147483648 | bytes 18874368 | tf_op jit(solution)/shard_map/exchange/pallas_call | solution.py:442
  52.5 2.9 %publish.1 = (bf16[16,32,512]{2,1,0:T(8,128)(2,1)}, f32[16,32,512]{2,1,0:T(8,128)}, f32[16,32,512]{2,1,0:T(8,128)}, f32[2,512,512]{2,1,0:T(8,128)}, f32[2,512,512]{2,1,0:T(8,128)}) custom-call(bf16[16,2,32,512]{3,2,1,0:T(8,128)(2,1)S(1)} %get-tuple-element.12.returned, f32[16,128]{1,0:T(8,128)S(1)} %get-tuple-element.13.graft, ...), custom_call_target="tpu_custom_call" | custom-call | tf_op jit(solution)/shard_map/publish/pallas_call | solution.py:572

commit v11 on v9

--- a/solution.py
+++ b/solution.py
@@ -12,6 +12,7 @@
 I32 = jnp.int32
 PARTS = ((0, 0, 1), (0, 1, 1), (0, 2, 2), (1, 0, 2), (1, 2, 1), (1, 3, 1))
 CHUNKS = len(PARTS)
+LATE = (CHUNKS - 2, CHUNKS - 1)
 SIDE = 4
 OFFSETS = (
     *((2, 2), (2, 1), (2, -1), (1, 2), (-1, 2), (2, 0), (0, 2)),
@@ -274,21 +275,32 @@
     def strip_part(k):
         return pl.ds(pl.multiple_of(rank * strip + PARTS[k][0] * height, height), height)
 
-    def to_owners(k):
+    def to_owners(k, only=None):
+        which = range(slots) if only is None else (only,)
+
         def visit(target):
-            for slot in range(slots):
+            for slot in which:
                 outgoing[k][target, slot] = reduced[k][block_of(target * slots + slot)]
+            if only is None:
+                src, dst = outgoing[k].at[target], block.at[:, strip_part(k), cols(k)]
+            else:
+                src, dst = outgoing[k].at[target, only], block.at[only, strip_part(k), cols(k)]
             pltpu.make_async_remote_copy(
-                src_ref=outgoing[k].at[target],
-                dst_ref=block.at[:, strip_part(k), cols(k)],
-                send_sem=owner_send.at[k],
-                recv_sem=owner_recv.at[k],
+                src_ref=src,
+                dst_ref=dst,
+                send_sem=owner_send.at[k, which[0]],
+                recv_sem=owner_recv.at[k, which[0]],
                 device_id={"fsdp": target},
             ).start()
 
         each_target(visit)
-        for slot in range(slots):
+        for slot in which:
             block[slot, strip_part(k), cols(k)] = reduced[k][block_of(rank * slots + slot)]
+
+    def owner_messages(k, slot):
+        if k in LATE:
+            return outgoing[k].at[pl.ds(0, ranks - 1), slot]
+        return outgoing[k].at[pl.ds(0, ranks - 1)]
 
     def moments(k):
         step = 4
@@ -326,17 +338,24 @@
         if 1 <= k < CHUNKS - 2:
             moments(k - 1)
         finish(k)
-        to_owners(k)
+        to_owners(k, 0 if k in LATE else None)
+    for slot in range(1, slots):
+        for k in LATE:
+            to_owners(k, slot)
     for k in range(CHUNKS - 3, CHUNKS):
         moments(k)
 
     def arrived(ref, sem):
         pltpu.make_async_copy(ref, ref, sem).wait()
 
-    for k in chunks:
-        arrived(outgoing[k].at[pl.ds(0, ranks - 1)], owner_recv.at[k])
     loads[0].wait()
     loads[1].wait()
+
+    def owners_have(slot):
+        for k in chunks:
+            if slot == 0 or k in LATE:
+                arrived(owner_messages(k, slot), owner_recv.at[k, slot])
+
 
     def precondition(slot):
         product = jnp.dot(root_left[slot], block[slot], preferred_element_type=F32)
@@ -372,8 +391,10 @@
 
     adam = jnp.sum(jnp.sum(jnp.sum(adam_sums[...], axis=0), axis=1), axis=1, keepdims=True)
     lane = lax.broadcasted_iota(I32, (8, 128), 1)
+    owners_have(0)
     precondition(0)
     send_back(0)
+    owners_have(1)
     precondition(1)
     tile = jnp.where(lane == 0, adam[:8], 0.0) + jnp.where(lane == 1, adam[8:], 0.0)
     for slot in range(slots):
@@ -414,7 +435,8 @@
     for copy in core_copies:
         copy.wait_send()
     for k in chunks:
-        arrived(outgoing[k].at[pl.ds(0, ranks - 1)], owner_send.at[k])
+        for slot in range(slots if k in LATE else 1):
+            arrived(owner_messages(k, slot), owner_send.at[k, slot])
     for slot in range(slots):
         arrived(direction.at[slot, pl.ds(0, (ranks - 1) * strip)], back_send.at[slot])
     arrived(all_sums.at[pl.ds(0, ranks - 1)], sums_send)
@@ -474,8 +496,8 @@
             dma((5,)),
             dma((CHUNKS, 6)),
             dma((CHUNKS, 6)),
-            dma((CHUNKS,)),
-            dma((CHUNKS,)),
+            dma((CHUNKS, slots)),
+            dma((CHUNKS, slots)),
             dma((slots,)),
             dma((slots,)),
             dma,

time: 55.5 us -> 55.2 us (level)
  no operation moved by 1% of the time
where the time goes in v11:
time: 55.2 us; the launch traced here: 55.1 us
  Pallas kernels  54.5 us (99%)
  between operations  0.64 us (1%)
    pallas_call x1, Pallas kernels, exchange(): pl.pallas_call(exchange_kernel, out_shape=(pltpu.VMEM((ranks, slots, stri...  51.6 us
    pallas_call x1, Pallas kernels, publish(): pl.pallas_call(publish_kernel, out_shape=[jax.ShapeDtypeStruct(*shape) fo...  2.86 us

profile of v11, /device:TPU:0, one launch (start us, length us, event | category | flops | bytes accessed | tf_op | source)
XLA Modules:
  0.0 55.1 jit_solution(12571147983658167979)
XLA Ops:
  0.6 51.6 %exchange.1 = (bf16[16,2,32,512]{3,2,1,0:T(8,128)(2,1)S(1)}, f32[16,128]{1,0:T(8,128)S(1)}, s32[8,128]{1,0:T(8,128)S(1)}, f32[16,32,512]{2,1,0:T(8,128)S(1)}, f3...) custom-call(s32[1,128]{1,0:T(1,128)} %bitcast.3, ...), custom_call_target="tpu_custom_call" | custom-call | flops 2147483648 | bytes 18874368 | tf_op jit(solution)/shard_map/exchange/pallas_call | solution.py:454
  52.3 2.9 %publish.1 = (bf16[16,32,512]{2,1,0:T(8,128)(2,1)}, f32[16,32,512]{2,1,0:T(8,128)}, f32[16,32,512]{2,1,0:T(8,128)}, f32[2,512,512]{2,1,0:T(8,128)}, f32[2,512,512]{2,1,0:T(8,128)}) custom-call(bf16[16,2,32,512]{3,2,1,0:T(8,128)(2,1)S(1)} %get-tuple-element.12.returned, f32[16,128]{1,0:T(8,128)S(1)} %get-tuple-element.13.graft, ...), custom_call_target="tpu_custom_call" | custom-call | tf_op jit(solution)/shard_map/publish/pallas_call | solution.py:578

commit v12 on v11

--- a/solution.py
+++ b/solution.py
@@ -342,8 +342,6 @@
     for slot in range(1, slots):
         for k in LATE:
             to_owners(k, slot)
-    for k in range(CHUNKS - 3, CHUNKS):
-        moments(k)
 
     def arrived(ref, sem):
         pltpu.make_async_copy(ref, ref, sem).wait()
@@ -389,13 +387,15 @@
             device_id={"fsdp": target},
         ).start()
 
-    adam = jnp.sum(jnp.sum(jnp.sum(adam_sums[...], axis=0), axis=1), axis=1, keepdims=True)
     lane = lax.broadcasted_iota(I32, (8, 128), 1)
     owners_have(0)
     precondition(0)
     send_back(0)
+    for k in range(CHUNKS - 3, CHUNKS):
+        moments(k)
     owners_have(1)
     precondition(1)
+    adam = jnp.sum(jnp.sum(jnp.sum(adam_sums[...], axis=0), axis=1), axis=1, keepdims=True)
     tile = jnp.where(lane == 0, adam[:8], 0.0) + jnp.where(lane == 1, adam[8:], 0.0)
     for slot in range(slots):
         tile = tile + jnp.where(lane == 2 + slot, squares(slot), 0.0)

time: 55.2 us -> 55.2 us (level)
  no operation moved by 1% of the time
where the time goes in v12:
time: 55.2 us; the launch traced here: 55.1 us
  Pallas kernels  54.5 us (99%)
  between operations  0.64 us (1%)
    pallas_call x1, Pallas kernels, exchange(): pl.pallas_call(exchange_kernel, out_shape=(pltpu.VMEM((ranks, slots, stri...  51.6 us
    pallas_call x1, Pallas kernels, publish(): pl.pallas_call(publish_kernel, out_shape=[jax.ShapeDtypeStruct(*shape) fo...  2.86 us

profile of v12, /device:TPU:0, one launch (start us, length us, event | category | flops | bytes accessed | tf_op | source)
XLA Modules:
  0.0 55.1 jit_solution(6489783290486039236)
XLA Ops:
  0.6 51.6 %exchange.1 = (bf16[16,2,32,512]{3,2,1,0:T(8,128)(2,1)S(1)}, f32[16,128]{1,0:T(8,128)S(1)}, s32[8,128]{1,0:T(8,128)S(1)}, f32[16,32,512]{2,1,0:T(8,128)S(1)}, f3...) custom-call(s32[1,128]{1,0:T(1,128)} %bitcast.3, ...), custom_call_target="tpu_custom_call" | custom-call | flops 2147483648 | bytes 18874368 | tf_op jit(solution)/shard_map/exchange/pallas_call | solution.py:454
  52.3 2.9 %publish.1 = (bf16[16,32,512]{2,1,0:T(8,128)(2,1)}, f32[16,32,512]{2,1,0:T(8,128)}, f32[16,32,512]{2,1,0:T(8,128)}, f32[2,512,512]{2,1,0:T(8,128)}, f32[2,512,512]{2,1,0:T(8,128)}) custom-call(bf16[16,2,32,512]{3,2,1,0:T(8,128)(2,1)S(1)} %get-tuple-element.12.returned, f32[16,128]{1,0:T(8,128)S(1)} %get-tuple-element.13.graft, ...), custom_call_target="tpu_custom_call" | custom-call | tf_op jit(solution)/shard_map/publish/pallas_call | solution.py:578

commit v13 on v11

--- a/solution.py
+++ b/solution.py
@@ -15,8 +15,8 @@
 LATE = (CHUNKS - 2, CHUNKS - 1)
 SIDE = 4
 OFFSETS = (
-    *((2, 2), (2, 1), (2, -1), (1, 2), (-1, 2), (2, 0), (0, 2)),
-    *((1, 1), (-1, -1), (1, -1), (-1, 1), (1, 0), (-1, 0), (0, 1), (0, -1)),
+    *((2, 0), (-1, -1), (0, 2), (1, -1), (2, 1), (0, -1), (-1, 2), (1, 0)),
+    *((2, 2), (-1, 0), (1, 2), (0, 1), (2, -1), (-1, 1), (1, 1)),
 )
 
 

time: 55.2 us -> 55.9 us (1.013)
  Pallas kernels: 54.5 us -> 55.2 us
    pallas_call x1, Pallas kernels: 51.6 us -> 52.3 us  [exchange(): pl.pallas_call(exchange_kernel, out_shape=(pltpu.VMEM((ranks, slots, stri...]
where the time goes in v13:
time: 55.9 us; the launch traced here: 55.8 us
  Pallas kernels  55.2 us (99%)
  between operations  0.64 us (1%)
    pallas_call x1, Pallas kernels, exchange(): pl.pallas_call(exchange_kernel, out_shape=(pltpu.VMEM((ranks, slots, stri...  52.3 us
    pallas_call x1, Pallas kernels, publish(): pl.pallas_call(publish_kernel, out_shape=[jax.ShapeDtypeStruct(*shape) fo...  2.86 us

profile of v13, /device:TPU:0, one launch (start us, length us, event | category | flops | bytes accessed | tf_op | source)
XLA Modules:
  0.0 55.8 jit_solution(811922896691429066)
XLA Ops:
  0.6 52.3 %exchange.1 = (bf16[16,2,32,512]{3,2,1,0:T(8,128)(2,1)S(1)}, f32[16,128]{1,0:T(8,128)S(1)}, s32[8,128]{1,0:T(8,128)S(1)}, f32[16,32,512]{2,1,0:T(8,128)S(1)}, f3...) custom-call(s32[1,128]{1,0:T(1,128)} %bitcast.3, ...), custom_call_target="tpu_custom_call" | custom-call | flops 2147483648 | bytes 18874368 | tf_op jit(solution)/shard_map/exchange/pallas_call | solution.py:454
  52.9 2.9 %publish.1 = (bf16[16,32,512]{2,1,0:T(8,128)(2,1)}, f32[16,32,512]{2,1,0:T(8,128)}, f32[16,32,512]{2,1,0:T(8,128)}, f32[2,512,512]{2,1,0:T(8,128)}, f32[2,512,512]{2,1,0:T(8,128)}) custom-call(bf16[16,2,32,512]{3,2,1,0:T(8,128)(2,1)S(1)} %get-tuple-element.12.returned, f32[16,128]{1,0:T(8,128)S(1)} %get-tuple-element.13.graft, ...), custom_call_target="tpu_custom_call" | custom-call | tf_op jit(solution)/shard_map/publish/pallas_call | solution.py:578
